TPU v7x, 128 devices: a whole 4x4x4 slice. The times are simulated.
128 devices in a mesh: req: 4 (over x), grp: 32 (over z, y, core).
Axes of the slice: x: 4, y: 4, z: 4, core: 2. Of those that a mesh axis runs over, the one named last changes fastest.
Arguments:
- rows_in: bfloat16 [4, 160, 8192], P('req'), may hold values from -6 to 6
- norm_gain: float32 [8192], replicated, may hold values from 0.5 to 1.5
- w_query: bfloat16 [8192, 8192], P(None, 'grp'), may hold values from -0.0625 to 0.0625
- w_keyval: bfloat16 [8192, 2048], P(None, 'grp'), may hold values from -0.0625 to 0.0625
- w_out: bfloat16 [8192, 8192], P(None, 'grp'), may hold values from -0.0625 to 0.0625
- page_pool: bfloat16 [32, 512, 2048], P('req', 'grp'), may hold values from -68 to 68
- stretch_ids: int32 [4, 4], replicated, may hold values from 0 to 31, as said below
- page_slot: int32 [32], replicated, may hold values from 0 to 31, as said below
- picked: int32 [4, 4, 24], replicated, may hold values from 0 to 511, as said below
- question_len: int32 [4], replicated, may hold values from 1 to 64
Outputs:
- attn_out: bfloat16 [4, 160, 8192], P('req', None, 'grp')
- joined_pool: bfloat16 [32, 512, 2048], P('req', 'grp')
Inputs may be any that keep to these rules, and one draw needn't show every extreme that they name: page_slot is a permutation. All ids in stretch_ids are distinct; of each request's 4 passages, exactly 1 has page_slot // 8 equal to each holder index. `picked`: the 24 positions of one passage are distinct.
All inputs are finite; a program needn't handle non-finite values.
Results may differ from a plain program's by a relative error of at most 0.0065.
The roundings to bfloat16 on the way count: a program that leaves them out, or rounds other values in their place, can miss the bound.
Values may be sent and summed in bfloat16 or wider, within the bound.
A program may use at most 64 MiB of HBM per device.

v0:
```python
import jax
import jax.numpy as jnp
from jax import lax
from jax.sharding import PartitionSpec as P

HQ = 64
KVH = 8
HD = 128


EPS = 1e-05


def token_parts(query, keys, visible):
    row_count = query.shape[0]
    group = HQ // KVH
    key_count = keys.shape[0]
    key_heads = keys[:, : KVH * HD].reshape(key_count, KVH, HD)
    val_heads = keys[:, KVH * HD :].astype(jnp.float32).reshape(key_count, KVH, HD)
    query_heads = query.reshape(row_count, KVH, group, HD)
    scores = jnp.einsum(
        "rhgd,khd->rhgk", query_heads, key_heads, preferred_element_type=jnp.float32
    ) * (1.0 / float(HD) ** 0.5)
    mask_full = visible[:, None, None, :]
    scores = jnp.where(mask_full, scores, -1e30)
    peak = jnp.max(scores, axis=-1)
    weights = jnp.where(mask_full, jnp.exp(scores - peak[..., None]), 0.0)
    total = jnp.sum(weights, axis=-1)
    partial_value = jnp.einsum(
        "rhgk,khd->rhgd", weights, val_heads, precision=lax.Precision.HIGHEST
    )
    return (
        peak.reshape(row_count, HQ),
        total.reshape(row_count, HQ),
        partial_value.reshape(row_count, HQ * HD),
    )


def local(
    rows_in,
    norm_gain,
    w_query,
    w_keyval,
    w_out,
    page_pool,
    stretch_ids,
    page_slot,
    picked,
    question_len,
):
    req_count = lax.axis_size("req")
    grp_count = lax.axis_size("grp")
    own_request = lax.axis_index("req")
    own_member = lax.axis_index("grp")
    pool_here, block_len, key_width = page_pool.shape
    span_count = stretch_ids.shape[1]
    per_holder = span_count // req_count
    recompute = picked.shape[2]
    row_count = rows_in.shape[1]
    leading = span_count * recompute
    question_slots = row_count - leading
    span_tok = block_len * grp_count
    context = span_count * span_tok
    inputs = rows_in[0].astype(jnp.float32)
    normed = (
        inputs * lax.rsqrt(jnp.mean(inputs * inputs, axis=-1, keepdims=True) + EPS) * norm_gain
    ).astype(jnp.bfloat16)
    query_part = jnp.dot(normed, w_query, preferred_element_type=jnp.float32).astype(jnp.bfloat16)
    keyval_part = jnp.dot(normed, w_keyval, preferred_element_type=jnp.float32).astype(jnp.bfloat16)
    fresh = lax.all_gather(keyval_part, "grp", axis=1, tiled=True)
    positions = page_slot[stretch_ids]
    holder = positions // pool_here
    local_slot = positions % pool_here
    holder_ids = jnp.arange(req_count, dtype=jnp.int32)
    same_holder = holder[:, :, None] == holder_ids[None, None, :]
    order_all = jnp.cumsum(same_holder.astype(jnp.int32), axis=1) - 1
    order_in = jnp.sum(jnp.where(same_holder, order_all, 0), axis=-1)
    slot_ids = jnp.arange(per_holder, dtype=jnp.int32)
    held_here = holder == own_request
    matches = held_here[:, :, None] & (order_in[:, :, None] == slot_ids[None, None, :])
    send_slots = jnp.sum(jnp.where(matches, local_slot[:, :, None], 0), axis=1)
    own_positions = lax.dynamic_index_in_dim(positions, own_request, 0, keepdims=False)
    own_holder = lax.dynamic_index_in_dim(holder, own_request, 0, keepdims=False)
    own_order = lax.dynamic_index_in_dim(order_in, own_request, 0, keepdims=False)
    whole_pool = lax.all_gather(page_pool, "req", axis=0, tiled=True)
    blocks = whole_pool[own_positions]
    own_picked = lax.dynamic_index_in_dim(picked, own_request, 0, keepdims=False)
    token_pos = own_member * block_len + jnp.arange(block_len, dtype=jnp.int32)
    onehot = own_picked[:, None, :] == token_pos[None, :, None]
    fresh_context = fresh[:leading].reshape(span_count, recompute, key_width)
    replaced = jnp.einsum(
        "cbr,crk->cbk",
        onehot.astype(jnp.bfloat16),
        fresh_context,
        preferred_element_type=jnp.float32,
    ).astype(jnp.bfloat16)
    joined = jnp.where(jnp.any(onehot, axis=-1)[:, :, None], replaced, blocks)
    own_length = lax.dynamic_index_in_dim(question_len, own_request, 0, keepdims=False)
    question_local = question_slots // grp_count
    question_keys = lax.dynamic_index_in_dim(
        fresh[leading:].reshape(question_local, grp_count, key_width), own_member, 1, keepdims=False
    )
    question_index = jnp.arange(question_local, dtype=jnp.int32) * grp_count + own_member
    span_base = (jnp.arange(span_count, dtype=jnp.int32) * span_tok)[:, None]
    key_pos = jnp.concatenate(
        [(span_base + token_pos[None, :]).reshape(-1), context + question_index]
    )
    key_live = jnp.concatenate(
        [jnp.ones((span_count * block_len,), dtype=bool), question_index < own_length]
    )
    keys = jnp.concatenate([joined.reshape(-1, key_width), question_keys], axis=0)
    query_pos = jnp.concatenate(
        [
            (span_base + own_picked).reshape(-1),
            context + jnp.arange(question_slots, dtype=jnp.int32),
        ]
    )
    visible = (key_pos[None, :] <= query_pos[:, None]) & key_live[None, :]
    query = lax.all_gather(query_part, "grp", axis=1, tiled=True)
    peak, total, partial_value = token_parts(query, keys, visible)
    peak_all = lax.pmax(peak.astype(jnp.bfloat16), "grp").astype(peak.dtype)
    factor = jnp.exp(peak - peak_all)
    scaled_total = total * factor
    scaled_part = (partial_value.reshape(row_count, HQ, HD) * factor[:, :, None]).reshape(
        row_count, HQ * HD
    )
    share_total, share_part = (
        lax.psum_scatter(scaled_total, "grp", scatter_dimension=1, tiled=True),
        lax.psum_scatter(scaled_part, "grp", scatter_dimension=1, tiled=True),
    )
    head_share = share_total.shape[1]
    share_attention = (
        (share_part.reshape(row_count, head_share, HD) / share_total[:, :, None])
        .reshape(row_count, head_share * HD)
        .astype(jnp.bfloat16)
    )
    attention = lax.all_gather(share_attention, "grp", axis=1, tiled=True)
    projected = jnp.dot(attention, w_out, preferred_element_type=jnp.float32)
    valid = jnp.concatenate(
        [jnp.ones((leading,), dtype=bool), jnp.arange(question_slots, dtype=jnp.int32) < own_length]
    )
    attn_out = jnp.where(valid[:, None], projected, 0.0).astype(jnp.bfloat16)[None]
    back_match = (own_holder[None, None, :] == holder_ids[:, None, None]) & (
        own_order[None, None, :] == slot_ids[None, :, None]
    )
    span_index = jnp.sum(
        jnp.where(back_match, jnp.arange(span_count, dtype=jnp.int32)[None, None, :], 0), axis=-1
    )
    outgoing_back = joined[span_index.reshape(-1)].reshape(
        req_count, per_holder, block_len, key_width
    )
    returned = lax.all_to_all(outgoing_back, "req", split_axis=0, concat_axis=0, tiled=True)
    joined_pool = page_pool.at[send_slots.reshape(-1)].set(
        returned.reshape(-1, block_len, key_width)
    )
    return (attn_out, joined_pool)


def solution(mesh):
    in_specs = (
        P("req", None, None),
        P(),
        P(None, "grp"),
        P(None, "grp"),
        P(None, "grp"),
        P("req", "grp", None),
        P(),
        P(),
        P(),
        P(),
    )
    out_specs = (P("req", None, "grp"), P("req", "grp", None))
    return jax.shard_map(local, mesh=mesh, in_specs=in_specs, out_specs=out_specs, check_vma=False)
```

profile of v0, /device:TPU:1, one launch (start us, length us, event | category | flops | bytes accessed | tf_op | source)
XLA Modules:
  0.0 437.3 jit_solution(4639870789681291784)
XLA Ops:
  7.2 0.0 copy-start
  7.2 0.0 all-gather.4.cloned.1.call-start
  7.2 2.0 copy.72
  9.2 0.0 all-gather.4.cloned.1.call-update
  9.2 0.0 all-gather.6.cloned.1.call-start
  9.3 2.4 fusion
  11.6 4.5 %convolution_convert_fusion.1 = bf16[160,256]{1,0:T(8,128)(2,1)} fusion(bf16[8192,256]{1,0:T(8,128)(2,1)} %param.12, bf16[1,160,8192]{2,1,0:T(8,128)(2,1)} %param.10, f32[8192]{0:T(1024)} %param.11, f32[160]{0:T(256)S(1)} %add_rsqrt_fusion), kind=kOutput, calls=%fused_computation.27 | convolution fusion | flops 676372480 | bytes 6931072 | tf_op jit(solution)/shard_map/dot_general | solution.py:68
  16.2 0.0 all-gather.6.cloned.1.call-update
  16.2 0.0 reduce-scatter.2.cloned.1.call-start
  16.3 2.8 convolution_convert_fusion.2
  19.1 27.8 %all_gather.12 = bf16[160,2048]{0,1:T(8,128)(2,1)S(1)} all-gather(bf16[160,64]{0,1:T(8,128)(2,1)S(1)} %convolution_convert_fusion.2), channel_id=1, replica_groups=mesh['req'=4,'grp'=32] {'grp'}, dimensions={1}, use_global_device_ids=true | all-gather | bytes 675840 | tf_op jit(solution)/shard_map/all_gather | solution.py:70
  46.9 0.2 slice.23
  47.2 0.1 add.150
  47.2 0.1 add.151
  47.3 0.1 broadcast_add_fusion
  47.4 0.1 add.146
  47.5 0.1 reshape.285
  47.6 0.6 dynamic_slice.24
  48.2 0.1 squeeze.22
  48.3 0.7 gather_fusion
  48.9 0.1 reshape.284
  49.0 0.1 fusion.27
  49.2 0.2 copy.34
  49.4 0.2 copy.33
  49.6 0.6 fusion.37
  50.2 0.1 concatenate.19
  50.3 0.2 select_reduce_fusion
  50.6 0.1 pad_add_fusion.1
  50.6 0.1 pad_add_fusion
  50.7 0.1 select_reduce_fusion.1
  50.9 0.2 compare_reduce_fusion
  51.1 0.1 compare_and_fusion
  51.2 0.0 all-gather.4.cloned.1.call-done
  51.2 2.2 gather_fusion.1
  53.4 0.3 fusion.14
  53.8 39.7 %all-gather.6.cloned.1.call-done = bf16[160,8192]{1,0:T(8,128)(2,1)} async-done(((bf16[160,256]{1,0:T(8,128)(2,1)}), bf16[160,8192]{1,0:T(8,128)(2,1)}) %all-gather.6.cloned.1.call-update) | async-done | bytes 2621456 | tf_op jit(solution)/shard_map/all_gather | solution.py:119
  93.5 2.5 copy.51
  96.0 5.4 %fusion.3 = (f32[160,8,8]{0,2,1:T(8,128)S(1)}, f32[8,66,160,8]{2,1,3,0:T(8,128)}) fusion(pred[160,66]{0,1:T(8,128)(4,1)S(1)} %compare_and_fusion, bf16[160,8,8,128]{3,2,1,0:T(8,128)(2,1)S(1)} %bitcast.96, bf16[66,8,128,1]{2,1,0,3:T(8,128)(2,1)S(1)} %slice_bitcast_fusion), kind=kOutput, calls=%fused_computation.12 | convolution fusion | flops 175032320 | bytes 5511488 | tf_op jit(solution)/shard_map/rhgd,khd->rhgk/dot_general | solution.py:21
  101.4 121.1 %pmax.7 = bf16[160,64]{0,1:T(8,128)(2,1)S(1)} all-reduce(bf16[160,64]{0,1:T(8,128)(2,1)S(1)} %bitcast_convert_fusion), channel_id=1, replica_groups=mesh['req'=4,'grp'=32] {'grp'}, use_global_device_ids=true, to_apply=%region_3.4 | all-reduce | flops 10240 | bytes 40960 | tf_op jit(solution)/shard_map/pmax | solution.py:121
  222.5 3.7 fusion.4
  226.2 0.1 copy.39
  226.3 7.3 %fusion.8 = f32[160,8,8,128]{3,0,2,1:T(8,128)S(1)} fusion(f32[8,66,160,8]{2,1,3,0:T(8,128)} %get-tuple-element.7, f32[160,8,8]{0,2,1:T(8,128)S(1)} %get-tuple-element.6, pred[160,66]{0,1:T(8,128)(4,1)S(1)} %compare_and_fusion, bf16[66,8,128,1]{2,1,0,3:T(8,128)(2,1)S(1)} %slice_bitcast_fusion.1), kind=kOutput, calls=%fused_computation.17 | convolution fusion | flops 1040793600 | bytes 8132928 | tf_op jit(solution)/shard_map/rhgk,khd->rhgd/dot_general | solution.py:29
  233.6 3.0 copy.38
  236.7 1.7 mul.68
  238.4 12.0 %bitcast_multiply_fusion = f32[160,8192]{1,0:T(8,128)} fusion(f32[20,8,64,128]{3,2,1,0:T(8,128)S(1)} %bitcast.95, f32[20,8,64,128]{3,2,1,0:T(8,128)S(1)} %bitcast.94), kind=kLoop, calls=%fused_computation.9 | loop fusion | flops 1310720 | bytes 15728640 | tf_op jit(solution)/shard_map/mul | solution.py:124
  250.4 0.0 reduce-scatter.2.cloned.1.call-update
  250.5 0.0 all-gather.8.cloned.1.call-start
  250.5 0.6 copy-done.8
  251.1 0.6 dynamic-slice
  252.3 124.2 %all-reduce.2 = f32[160,64]{0,1:T(8,128)S(1)} all-reduce(f32[160,64]{0,1:T(8,128)S(1)} %get-tuple-element.2), channel_id=3, replica_groups=mesh['req'=4,'grp'=32] {'grp'}, use_global_device_ids=true, to_apply=%region_6.7.clone | all-reduce | flops 10240 | bytes 81920
  376.6 0.1 copy.40
  376.7 0.0 reduce-scatter.2.cloned.1.call-done
  376.7 0.2 div.31
  376.9 1.6 fusion.19
  378.5 0.0 all-gather.8.cloned.1.call-update
  378.6 0.6 iota_compare_fusion.2
  379.1 0.1 concatenate.15
  379.2 0.1 fusion.29
  379.4 1.3 gather_fusion.2
  380.6 4.0 all-to-all-start
  384.6 5.5 %all-to-all-done = bf16[4,1,16,2048]{3,2,1,0:T(8,128)(2,1)S(1)} async-done(((bf16[4,1,16,2048]{3,2,1,0:T(8,128)(2,1)}), bf16[4,1,16,2048]{3,2,1,0:T(8,128)(2,1)S(1)}, u32[]{:S(2)}, u32[]{:S(2)}) %all-to-all-start) | async-done | bytes 262176 | tf_op jit(solution)/shard_map/all_to_all | solution.py:152
  390.1 0.7 scatter_fusion
  390.8 35.5 %all-gather.8.cloned.1.call-done = bf16[160,8192]{1,0:T(8,128)(2,1)} async-done(((bf16[160,256]{1,0:T(8,128)(2,1)}), bf16[160,8192]{1,0:T(8,128)(2,1)}) %all-gather.8.cloned.1.call-update) | async-done | bytes 2621456 | tf_op jit(solution)/shard_map/all_gather | solution.py:137
  426.3 4.5 %fusion.16 = bf16[1,160,256]{2,1,0:T(8,128)(2,1)} fusion(bf16[160,8192]{1,0:T(8,128)(2,1)} %all-gather.8.cloned.1.call-done, bf16[8192,256]{1,0:T(8,128)(2,1)} %param.14, pred[160]{0:T(512)(128)(4,1)S(1)} %concatenate.15), kind=kOutput, calls=%fused_computation.28 | convolution fusion | flops 671170560 | bytes 6897824 | tf_op jit(solution)/shard_map/dot_general | solution.py:138
  (45 shorter events, 0.4 us)
Async XLA Ops:
  7.2 9.1 %copy-start = (bf16[8192,64]{0,1:T(8,128)(2,1)S(1)}, bf16[8192,64]{0,1:T(8,128)(2,1)}, u32[]{:S(2)}) copy-start(bf16[8192,64]{0,1:T(8,128)(2,1)} %param.13) | copy-start | bytes 3145732
  7.2 44.0 %all-gather.4.cloned.1.call-start = ((), (), s32[]{:S(2)}) async-start(), calls=%async_computation.2 | async-start | bytes 2621440 | tf_op jit(solution)/shard_map/all_gather | solution.py:85
  9.2 84.3 %all-gather.6.cloned.1.call-start = ((), (), s32[]{:S(2)}) async-start(), calls=%async_computation.3 | async-start | bytes 2703360 | tf_op jit(solution)/shard_map/all_gather | solution.py:119
  11.6 4.7 %copy-start.6 = (f32[8192]{0:T(1024)S(1)}, f32[8192]{0:T(1024)}, u32[]{:S(2)}) copy-start(f32[8192]{0:T(1024)} %param.11) | copy-start | bytes 98308
  16.2 31.3 %copy-start.5 = (s32[4,4]{1,0:T(4,128)S(1)}, s32[4,4]{1,0:T(4,128)}, u32[]{:S(2)}) copy-start(s32[4,4]{1,0:T(4,128)} %param.16) | copy-start | bytes 196
  16.2 31.4 %copy-start.7 = (s32[4]{0:T(128)S(1)}, s32[4]{0:T(128)}, u32[]{:S(2)}) copy-start(s32[4]{0:T(128)} %param.19) | copy-start | bytes 52
  16.2 32.0 %copy-start.4 = (s32[4,4,24]{2,1,0:T(4,128)S(1)}, s32[4,4,24]{2,1,0:T(4,128)}, u32[]{:S(2)}) copy-start(s32[4,4,24]{2,1,0:T(4,128)} %param.18) | copy-start | bytes 4612
  16.2 32.1 %copy-start.1 = (s32[32]{0:T(128)S(1)}, s32[32]{0:T(128)}, u32[]{:S(2)}) copy-start(s32[32]{0:T(128)} %param.17) | copy-start | bytes 388
  16.2 360.5 %reduce-scatter.2.cloned.1.call-start = ((), (), s32[]{:S(2)}) async-start(), calls=%async_computation.4 | async-start | bytes 5406720 | tf_op jit(solution)/shard_map/reduce_scatter | solution.py:129
  250.4 0.7 copy-start.8
  250.4 139.7 %copy-start.2 = (bf16[8,16,2048]{2,1,0:T(8,128)(2,1)S(1)}, bf16[8,16,2048]{2,1,0:T(8,128)(2,1)}, u32[]{:S(2)}) copy-start(bf16[8,16,2048]{2,1,0:T(8,128)(2,1)} %copy.72) | copy-start | bytes 1572868
  250.5 175.8 %all-gather.8.cloned.1.call-start = ((), (), s32[]{:S(2)}) async-start(), calls=%async_computation.5 | async-start | bytes 2703360 | tf_op jit(solution)/shard_map/all_gather | solution.py:137
  380.6 9.5 %all-to-all-start = ((bf16[4,1,16,2048]{3,2,1,0:T(8,128)(2,1)}), bf16[4,1,16,2048]{3,2,1,0:T(8,128)(2,1)S(1)}, u32[]{:S(2)}, u32[]{:S(2)}) async-start(bf16[4,1,16,2048]{3,2,1,0:T(8,128)(2,1)} %bitcast.23), calls=%async_computation.1 | async-start | bytes 524288 | tf_op jit(solution)/shard_map/all_to_all | solution.py:152
  390.8 39.9 %copy-start.3 = (bf16[8,16,2048]{2,1,0:T(8,128)(2,1)}, bf16[8,16,2048]{2,1,0:T(8,128)(2,1)S(1)}, u32[]{:S(2)}) copy-start(bf16[8,16,2048]{2,1,0:T(8,128)(2,1)S(1)} %scatter_fusion) | copy-start | bytes 1572868
Sparse Core Ops, SparseCore 0:
  10.3 34.0 all-gather.3
  47.1 46.4 all-gather.5
  250.6 84.3 reduce-scatter.1
  378.7 47.5 all-gather.7
where the time goes:
time: 438 us; the launch traced here: 437 us
  blocking collectives  273 us (62%)
  waiting for transfers between devices  80.8 us (18%)
  matrix products  24.8 us (6%)
  other arithmetic  22.1 us (5%)
  local copies, waits for them, and re-layouts  17.6 us (4%)
  between operations  14.7 us (3%)
    unnamed x1, blocking collectives  124 us
    pmax x1, blocking collectives, local(): peak_all = lax.pmax(peak.astype(jnp.bfloat16), 'grp').astype(peak.dtype)  121 us
    all_gather x1, waiting for transfers between devices, local(): query = lax.all_gather(query_part, 'grp', axis=1, tiled=True)  39.7 us
    all_gather x1, waiting for transfers between devices, local(): attention = lax.all_gather(share_attention, 'grp', axis=1, tiled=True)  35.5 us
    all_gather x1, blocking collectives, local(): fresh = lax.all_gather(keyval_part, 'grp', axis=1, tiled=True)  27.8 us
    mul x1, other arithmetic, local(): partial_value.reshape(row_count, HQ, HD) * factor[:, :, None]  12 us
  transfers between devices with their start and end apart: 5, of which 3 were waited for; matrix products, arithmetic and copies ran while one was open for 5% of the time, Pallas kernels for 0%

commit v1 on v0

v1 whole, which is shorter than its diff:
```python
import functools

import jax
import jax.numpy as jnp
from jax import lax
from jax.experimental import pallas as pl
from jax.experimental.pallas import tpu as pltpu
from jax.sharding import PartitionSpec as P

MESH = pl.DeviceIdType.MESH
F32 = jnp.float32
BF16 = jnp.bfloat16
HD = 128
KVH = 8
ROWS = 160
RCH = 24
SPANS = 4
D = 8192
KEYS = 2048
EPS = 1e-05
SCALE = 1.0 / float(HD) ** 0.5
NEG = -1e30
FAR = 1e9
LINE = (0, 1, 3, 2)


def nt_dot(a, b):
    return lax.dot_general(a, b, (((1,), (1,)), ((), ())), preferred_element_type=F32)


def nn_dot(a, b):
    return jnp.dot(a, b, preferred_element_type=F32)


def by_index(index, values):
    low = jnp.where(index == 0, values[0], values[1])
    return jnp.where(index < 2, low, jnp.where(index == 2, values[2], values[3]))


def to_column(row):
    n = row.shape[1]
    eye = lax.broadcasted_iota(jnp.int32, (n, n), 0) == lax.broadcasted_iota(jnp.int32, (n, n), 1)
    return jnp.sum(jnp.where(eye, jnp.broadcast_to(row, (n, n)), 0.0), axis=1, keepdims=True)


def kernel(
    rows_hbm,
    gain_hbm,
    wq_hbm,
    wk_hbm,
    wo_hbm,
    pool_hbm,
    ids,
    slots,
    picked,
    qlen,
    out_ref,
    joined_hbm,
    rows_v,
    gain_v,
    nrm,
    wq_v,
    wk_v,
    wo_v,
    pool_v,
    joined_v,
    sx,
    rx,
    kv,
    kvp,
    fr,
    fk,
    q2,
    scores,
    peak,
    total,
    part,
    gath,
    acc,
    sj,
    rj1,
    rj,
    ld,
    xs_s,
    xs_r,
    zs_s,
    zs_r,
    cs_s,
    cs_r,
    fr_s,
    fr_r,
    js_s,
    js_r,
    jz_s,
    jz_r,
    g_s,
    g_r,
    gc_s,
    gc_r,
    out_sem,
):
    r = lax.axis_index("req")
    m = lax.axis_index("grp")
    z = lax.div(m, 8)
    y = lax.rem(lax.div(m, 2), 4)
    c = lax.rem(m, 2)
    chip = lax.div(m, 2)
    k = lax.div(m, 4)
    sib = (r, m + 1 - 2 * c)

    def load(src, dst, i):
        cp = pltpu.make_async_copy(src, dst, ld.at[i])
        cp.start()
        return cp

    def push(src, dst, send, recv, dev):
        pltpu.make_async_remote_copy(
            src_ref=src, dst_ref=dst, send_sem=send, recv_sem=recv, device_id=dev, device_id_type=MESH
        ).start()

    def wait_all(ref, sem):
        pltpu.make_async_copy(ref, ref, sem).wait()

    ld_pool = load(pool_hbm, pool_v, 0)
    ld_rows = [
        load(rows_hbm.at[0, pl.ds(32 * i, 32)], rows_v.at[pl.ds(32 * i, 32)], 1 + i) for i in range(5)
    ]
    ld_gain = load(gain_hbm, gain_v, 6)
    ld_wk = load(wk_hbm, wk_v.at[pl.ds(pl.multiple_of(64 * c, 64), 64)], 7)
    ld_wq = [
        load(wq_hbm.at[pl.ds(2048 * i, 2048)], wq_v.at[pl.ds(2048 * i, 2048)], 8 + i) for i in range(4)
    ]
    ld_wo = load(wo_hbm, wo_v, 12)

    barrier = pltpu.get_barrier_semaphore()

    def greet(d, carry):
        pl.semaphore_signal(barrier, inc=1, device_id=(r, lax.rem(m + d, 32)), device_id_type=MESH)
        return carry

    lax.fori_loop(1, 32, greet, 0)
    for d in range(1, 4):
        pl.semaphore_signal(barrier, inc=1, device_id=(lax.rem(r + d, 4), m), device_id_type=MESH)

    wk_v[pl.ds(pl.multiple_of(64 - 64 * c, 64), 64), :] = jnp.zeros((64, D), BF16)

    place = [[slots[ids[q, s]] for s in range(SPANS)] for q in range(4)]
    send_slot, send_span = [], []
    for q in range(4):
        slot_q, span_q = 0, 0
        for s in range(SPANS):
            here = (place[q][s] >> 3) == r
            slot_q = slot_q + jnp.where(here, place[q][s] & 7, 0)
            span_q = span_q + jnp.where(here, s, 0)
        send_slot.append(slot_q)
        send_span.append(span_q)
    own_place = [slots[ids[r, s]] for s in range(SPANS)]
    span_of = []
    for x in range(4):
        span_x = 0
        for s in range(SPANS):
            span_x = span_x + jnp.where((own_place[s] >> 3) == x, s, 0)
        span_of.append(span_x)

    ld_pool.wait()
    row = lax.broadcasted_iota(jnp.int32, (64, 128), 0)
    wanted = by_index(row >> 4, send_slot) * 16 + (row & 15)
    pick_page = jnp.where(lax.broadcasted_iota(jnp.int32, (64, 128), 1) == wanted, 1.0, 0.0).astype(BF16)
    for h in range(2 * KVH):
        piece = nn_dot(pick_page, pool_v[:, :, h * HD : (h + 1) * HD].reshape(128, HD)).astype(BF16)
        for q in range(4):
            sx[q, h % KVH, h // KVH] = piece[16 * q : 16 * (q + 1)]
    pl.semaphore_wait(barrier, 34)
    for d in (1, 3, 2):
        q = lax.rem(r + d, 4)
        push(sx.at[q], rx.at[r], xs_s.at[0], xs_r.at[d - 1], (q, m))

    def spread(src, x):
        def one(d, carry):
            t = lax.rem(chip + d, 16)
            push(
                src.at[lax.div(t, 2)],
                kv.at[c, chip, x],
                zs_s.at[0],
                zs_r.at[z],
                (r, 2 * t + c),
            )
            return carry

        pltpu.make_async_copy(src.at[k], kv.at[c, chip, x], zs_r.at[z]).start()
        lax.fori_loop(1, 16, one, 0)

    spread(sx.at[r], r)

    ld_gain.wait()
    for i in range(5):
        ld_rows[i].wait()

    def norm(i, carry):
        at = pl.ds(pl.multiple_of(32 * i, 32), 32)
        squares = jnp.zeros((32, 128), F32)
        for j in range(D // 128):
            v = rows_v[at, j * 128 : (j + 1) * 128].astype(F32)
            squares = squares + v * v
        mean = jnp.sum(squares, axis=1, keepdims=True) * (1.0 / D)
        inv = jnp.broadcast_to(lax.rsqrt(mean + EPS), (32, 128))
        for j in range(D // 128):
            v = rows_v[at, j * 128 : (j + 1) * 128].astype(F32)
            nrm[at, j * 128 : (j + 1) * 128] = (v * inv * gain_v[:, j * 128 : (j + 1) * 128]).astype(BF16)
        return carry

    lax.fori_loop(0, 5, norm, 0)

    ld_wk.wait()
    part[0:ROWS, :] = jnp.zeros((ROWS, HD), F32)

    def kv_step(i, carry):
        cols = pl.ds(pl.multiple_of(1024 * i, 1024), 1024)
        part[0:ROWS, :] += nt_dot(nrm[:, cols], wk_v[:, cols])
        return carry

    lax.fori_loop(0, 8, kv_step, 0)
    kvp[...] = part[0:ROWS, :].astype(BF16)
    head_to = lax.div(lax.rem(m, 16), 2)
    fr_slot = lax.div(m, 16) * 2 + c
    for i in range(4):
        t = 4 * head_to + i

        @pl.when(t == m)
        def _():
            pltpu.make_async_copy(kvp, fr.at[fr_slot], fr_r.at[0]).start()

        @pl.when(t != m)
        def _():
            push(kvp, fr.at[fr_slot], fr_s.at[0], fr_r.at[0], (r, t))

    for d in (1, 3, 2):
        x = lax.rem(r + 4 - d, 4)
        wait_all(rx.at[x], xs_r.at[d - 1])
        spread(rx.at[x], x)

    acc[...] = jnp.zeros((ROWS, 2 * HD), F32)
    for i in range(4):
        ld_wq[i].wait()

        def q_step(j, carry):
            at = pl.multiple_of(2048 * i + 1024 * j, 1024)
            acc[...] += nn_dot(nrm[:, pl.ds(at, 1024)], wq_v[pl.ds(at, 1024), :])
            return carry

        lax.fori_loop(0, 2, q_step, 0)
    q2[0:ROWS, :] = acc[:, 0:HD].astype(BF16)
    q2[ROWS : 2 * ROWS, :] = acc[:, HD : 2 * HD].astype(BF16)

    own_picked = picked[r].astype(F32)
    cols = [to_column(own_picked[s : s + 1, :]) + 512.0 * s for s in range(SPANS)]
    question = lax.broadcasted_iota(jnp.int32, (64, 1), 0).astype(F32)
    own_len = qlen[r].astype(F32)
    row_pos = jnp.concatenate(cols + [question + float(KEYS)], axis=0)
    key_col = jnp.concatenate(cols + [jnp.where(question < own_len, question + float(KEYS), FAR)], axis=0)
    eye = lax.broadcasted_iota(jnp.int32, (ROWS, 256), 0) == lax.broadcasted_iota(jnp.int32, (ROWS, 256), 1)
    fresh_pos = jnp.sum(jnp.where(eye, jnp.broadcast_to(key_col, (ROWS, 256)), 0.0), axis=0, keepdims=True)
    fresh_pos = jnp.where(lax.broadcasted_iota(jnp.int32, (1, 256), 1) < ROWS, fresh_pos, FAR)
    row_pos_b = jnp.broadcast_to(row_pos, (ROWS, 256))
    picked_b = row_pos_b[0 : SPANS * RCH]

    wait_all(fr, fr_r.at[0])
    row = lax.broadcasted_iota(jnp.int32, (SPANS * RCH, 256), 0)
    wanted = by_index(lax.div(row, RCH), span_of) * RCH + lax.rem(row, RCH)
    pick_rows = jnp.where(lax.broadcasted_iota(jnp.int32, (SPANS * RCH, 256), 1) == wanted, 1.0, 0.0).astype(BF16)
    by_holder = []
    for s in range(2):
        fk[s, 0:ROWS, :] = (fr[2 * s].astype(F32) + fr[2 * s + 1].astype(F32)).astype(BF16)
        fk[s, ROWS:256, :] = jnp.zeros((256 - ROWS, HD), BF16)
        by_holder.append(nn_dot(pick_rows, fk[s]))
    for x in range(4):
        sj[x] = jnp.concatenate([b[x * RCH : (x + 1) * RCH] for b in by_holder], axis=0).astype(BF16)
    for d in (1, 3, 2):
        x = lax.rem(r + d, 4)
        push(sj.at[x], rj1.at[r], js_s.at[0], js_r.at[d - 1], (x, m))
    rj1[r] = sj[r]

    def score(at, keys, key_pos):
        s = nt_dot(q2[...], keys) * SCALE
        seen = row_pos_b >= jnp.broadcast_to(key_pos, (ROWS, 256))
        for half in range(2):
            rows = slice(half * ROWS, (half + 1) * ROWS)
            masked = jnp.where(seen, s[rows], NEG)
            scores[at, rows, :] = masked
            peak[rows, :] = jnp.maximum(peak[rows, :], jnp.maximum(masked[:, :128], masked[:, 128:]))

    peak[...] = jnp.full((2 * ROWS, 128), NEG, F32)
    score(8, fk[0], fresh_pos)

    lane = lax.broadcasted_iota(jnp.int32, (1, 256), 1)
    lane_x = (lane >> 4) & 3
    span_lane = by_index(lane_x, span_of)
    lane_pos = span_lane * 512 + (lane >> 6) * 32 + (lane & 15)

    def page_keys(cc, zz):
        pos = (lane_pos + (zz * 128 + cc * 16)).astype(F32)
        same = picked_b == jnp.broadcast_to(pos, (SPANS * RCH, 256))
        gone = jnp.max(jnp.where(same, 1.0, 0.0), axis=0, keepdims=True)
        return jnp.where(gone > 0.5, FAR, pos)

    for d in (0, 1, 3, 2):
        zz = lax.rem(z + d, 4)
        group = kv.at[c, pl.ds(4 * zz, 4)]
        wait_all(group, zs_r.at[zz])
        push(group, group, cs_s.at[0], cs_r.at[zz], sib)

    def own_scores(zz, carry):
        keys = kv[c, pl.ds(4 * zz, 4), :, 0].reshape(256, HD)
        score(zz, keys, page_keys(c, zz))
        return carry

    lax.fori_loop(0, 4, own_scores, 0)

    for d in (1, 3, 2):
        x = lax.rem(r + 4 - d, 4)
        wait_all(rj1.at[x], js_r.at[d - 1])
    rj[k] = rj1[...]

    def spread_fresh(d, carry):
        t = lax.rem(k + d, 8)
        push(rj1, rj.at[k], jz_s.at[0], jz_r.at[0], (r, (2 * t + lax.rem(y, 2)) * 2 + c))
        return carry

    lax.fori_loop(1, 8, spread_fresh, 0)

    def sib_scores(zz, carry):
        wait_all(kv.at[1 - c, pl.ds(4 * zz, 4)], cs_r.at[zz])
        keys = kv[1 - c, pl.ds(4 * zz, 4), :, 0].reshape(256, HD)
        score(4 + zz, keys, page_keys(1 - c, zz))
        return carry

    lax.fori_loop(0, 4, sib_scores, 0)

    peak[...] = jnp.broadcast_to(jnp.max(peak[...], axis=1, keepdims=True), (2 * ROWS, 128))
    total[...] = jnp.zeros((2 * ROWS, 128), F32)
    part[...] = jnp.zeros((2 * ROWS, HD), F32)

    def weigh(at, vals):
        top = peak[...]
        w0 = jnp.exp(scores[at, :, 0:128] - top)
        w1 = jnp.exp(scores[at, :, 128:256] - top)
        total[...] += w0 + w1
        part[...] += nn_dot(jnp.concatenate([w0, w1], axis=1).astype(BF16), vals)

    def page_values(i, carry):
        far = lax.div(i, 4)
        cc = c + far * (1 - 2 * c)
        zz = lax.rem(i, 4)
        weigh(i, kv[cc, pl.ds(4 * zz, 4), :, 1].reshape(256, HD))
        return carry

    lax.fori_loop(0, 8, page_values, 0)
    weigh(8, fk[1])
    att = part[...] / jnp.sum(total[...], axis=1, keepdims=True)
    gath[c, chip, :, 0:HD] = att[0:ROWS].astype(BF16)
    gath[c, chip, :, HD : 2 * HD] = att[ROWS : 2 * ROWS].astype(BF16)

    def chip_at(cc, df, ds):
        f = lax.rem(y * (1 - cc) + z * cc + df, 4)
        s = lax.rem(z * (1 - cc) + y * cc + ds, 4)
        return (4 * s + f) * (1 - cc) + (4 * f + s) * cc

    def forward(block, df, ds):
        ref = gath.at[c, block]
        push(ref, ref, g_s.at[0], g_r.at[block], (r, 2 * chip_at(c, df, ds) + c))

    def across(block):
        ref = gath.at[c, block]
        push(ref, ref, gc_s.at[0], gc_r.at[block], sib)

    def arrived(block):
        wait_all(gath.at[c, block], g_r.at[block])

    def project(cc, ds, wait):
        def one(df, carry):
            block = chip_at(cc, df, ds)
            if wait:
                wait_all(gath.at[cc, block], gc_r.at[block])
            at = pl.multiple_of((2 * block + cc) * 256, 256)
            acc[...] += nn_dot(gath[cc, block], wo_v[pl.ds(at, 256), :])
            return carry

        lax.fori_loop(0, 4, one, 0)

    for df, ds in ((1, 0), (3, 0), (2, 0), (0, 1), (0, 3)):
        forward(chip, df, ds)
    across(chip)
    acc[...] = jnp.zeros((ROWS, 2 * HD), F32)
    for df in (1, 3, 2):
        block = chip_at(c, df, 0)
        arrived(block)
        forward(block, 0, 1)
        forward(block, 0, 3)
        across(block)
    ld_wo.wait()
    project(c, 0, False)
    for df in LINE:
        for ds in (1, 3):
            block = chip_at(c, df, ds)
            arrived(block)
            if (ds == 3) == (df in (0, 2)):
                forward(block, 0, 4 - ds)
            across(block)
    project(1 - c, 0, True)
    project(c, 1, False)
    project(c, 3, False)

    wait_all(rj.at[pl.ds(0, 7)], jz_r.at[0])
    col = lax.broadcasted_iota(jnp.int32, (RCH, 192), 1)
    col_req = lax.div(col, 48)
    col_in = lax.rem(col, 48)
    row_in = lax.broadcasted_iota(jnp.int32, (RCH, 192), 0)
    target = jnp.zeros((1, 192), F32)
    low = (m * 16).astype(F32)
    for q in range(4):
        pq = picked[q].astype(F32)
        mine = jnp.zeros((1, RCH), F32)
        for s in range(SPANS):
            mine = mine + jnp.where(send_span[q] == s, pq[s : s + 1, :], 0.0)
        mine = mine - low
        mine = jnp.where((mine >= 0.0) & (mine < 16.0), mine + (send_slot[q] * 16).astype(F32), -1.0)
        fits = (col_req == q) & ((col_in == row_in) | (col_in == row_in + RCH))
        target = target + jnp.sum(
            jnp.where(fits, jnp.broadcast_to(to_column(mine), (RCH, 192)), 0.0), axis=0, keepdims=True
        )
    line = lax.broadcasted_iota(jnp.int32, (128, 192), 0).astype(F32)
    is_key = lax.rem(lax.broadcasted_iota(jnp.int32, (128, 192), 1), 48) < RCH
    match = line == jnp.broadcast_to(target, (128, 192))
    pick_key = jnp.where(match & is_key, 1.0, 0.0)
    pick_val = jnp.where(match & jnp.logical_not(is_key), 1.0, 0.0)
    hit = jnp.broadcast_to(jnp.max(pick_key, axis=1, keepdims=True), (128, HD)) > 0.5
    pick = jnp.concatenate([pick_key, pick_val], axis=0).astype(BF16)
    for h in range(KVH):
        new = nn_dot(pick, rj[h].reshape(192, HD))
        for s in range(2):
            at = slice(1024 * s + h * HD, 1024 * s + (h + 1) * HD)
            old = pool_v[:, :, at].astype(F32).reshape(128, HD)
            joined_v[:, :, at] = (
                jnp.where(hit, new[128 * s : 128 * (s + 1)], old).astype(BF16).reshape(8, 16, HD)
            )
    joined_out = pltpu.make_async_copy(joined_v, joined_hbm, out_sem.at[0])
    joined_out.start()

    project(1 - c, 1, True)
    project(1 - c, 3, True)
    for df in LINE:
        block = chip_at(c, df, 2)
        arrived(block)
        across(block)
    project(c, 2, False)
    project(1 - c, 2, True)
    live = lax.broadcasted_iota(jnp.int32, (ROWS, 2 * HD), 0) < SPANS * RCH + qlen[r]
    out_ref[0] = jnp.where(live, acc[...], 0.0).astype(BF16)

    joined_out.wait()
    wait_all(rx.at[pl.ds(0, 3)], xs_s.at[0])
    wait_all(kv.at[0, pl.ds(0, 15)], zs_s.at[0])
    wait_all(kv.at[0], cs_s.at[0])

    @pl.when(head_to == k)
    def _():
        wait_all(fr.at[pl.ds(0, 3)], fr_s.at[0])

    @pl.when(head_to != k)
    def _():
        wait_all(fr, fr_s.at[0])

    wait_all(rj1.at[pl.ds(0, 3)], js_s.at[0])
    wait_all(rj.at[pl.ds(0, 7)], jz_s.at[0])
    wait_all(gath.at[0, pl.ds(0, 15)], g_s.at[0])
    wait_all(gath.at[0], gc_s.at[0])


def local(
    rows_in, norm_gain, w_query, w_keyval, w_out, page_pool, stretch_ids, page_slot, picked, question_len
):
    any_spec = pl.BlockSpec(memory_space=pl.ANY)
    smem = pl.BlockSpec(memory_space=pltpu.SMEM)
    vmem = pl.BlockSpec(memory_space=pltpu.VMEM)
    sem = pltpu.SemaphoreType.DMA
    return pl.pallas_call(
        kernel,
        out_shape=(
            jax.ShapeDtypeStruct((1, ROWS, 2 * HD), BF16),
            jax.ShapeDtypeStruct(page_pool.shape, BF16),
        ),
        in_specs=[any_spec] * 6 + [smem, smem, vmem, smem],
        out_specs=(vmem, any_spec),
        scratch_shapes=[
            pltpu.VMEM((ROWS, D), BF16),
            pltpu.VMEM((1, D), F32),
            pltpu.VMEM((ROWS, D), BF16),
            pltpu.VMEM((D, 2 * HD), BF16),
            pltpu.VMEM((HD, D), BF16),
            pltpu.VMEM((D, 2 * HD), BF16),
            pltpu.VMEM((8, 16, 2048), BF16),
            pltpu.VMEM((8, 16, 2048), BF16),
            pltpu.VMEM((4, KVH, 2, 16, HD), BF16),
            pltpu.VMEM((4, KVH, 2, 16, HD), BF16),
            pltpu.VMEM((2, 16, 4, 2, 16, HD), BF16),
            pltpu.VMEM((ROWS, HD), BF16),
            pltpu.VMEM((4, ROWS, HD), BF16),
            pltpu.VMEM((2, 256, HD), BF16),
            pltpu.VMEM((2 * ROWS, HD), BF16),
            pltpu.VMEM((9, 2 * ROWS, 256), F32),
            pltpu.VMEM((2 * ROWS, 128), F32),
            pltpu.VMEM((2 * ROWS, 128), F32),
            pltpu.VMEM((2 * ROWS, HD), F32),
            pltpu.VMEM((2, 16, ROWS, 2 * HD), BF16),
            pltpu.VMEM((ROWS, 2 * HD), F32),
            pltpu.VMEM((4, 2 * RCH, HD), BF16),
            pltpu.VMEM((4, 2 * RCH, HD), BF16),
            pltpu.VMEM((KVH, 4, 2 * RCH, HD), BF16),
            sem((13,)),
            sem((1,)),
            sem((3,)),
            sem((1,)),
            sem((4,)),
            sem((1,)),
            sem((4,)),
            sem((1,)),
            sem((1,)),
            sem((1,)),
            sem((3,)),
            sem((1,)),
            sem((1,)),
            sem((1,)),
            sem((16,)),
            sem((1,)),
            sem((16,)),
            sem((1,)),
        ],
        compiler_params=pltpu.CompilerParams(
            collective_id=0, has_side_effects=True, vmem_limit_bytes=56 * 1024 * 1024
        ),
        name="joined_attention",
    )(
        rows_in,
        norm_gain.reshape(1, D),
        w_query,
        w_keyval.T,
        w_out,
        page_pool,
        stretch_ids,
        page_slot,
        picked,
        question_len,
    )


def solution(mesh):
    in_specs = (
        P("req", None, None),
        P(),
        P(None, "grp"),
        P(None, "grp"),
        P(None, "grp"),
        P("req", "grp", None),
        P(),
        P(),
        P(),
        P(),
    )
    out_specs = (P("req", None, "grp"), P("req", "grp", None))
    return jax.shard_map(local, mesh=mesh, in_specs=in_specs, out_specs=out_specs, check_vma=False)
```

time: 438 us -> 47.7 us (0.11)
  blocking collectives: 273 us -> 0 us
  waiting for transfers between devices: 80.8 us -> 0 us
  Pallas kernels: 0 us -> 43.4 us
  matrix products: 24.8 us -> 0 us
  other arithmetic: 22.1 us -> 0 us
  local copies, waits for them, and re-layouts: 17.6 us -> 3.41 us
  between operations: 14.7 us -> 0.64 us
    unnamed x1 -> x0, blocking collectives: 124 us -> none
    pmax x1 -> x0, blocking collectives: 121 us -> none  [local(): peak_all = lax.pmax(peak.astype(jnp.bfloat16), 'grp').astype(peak.dtype)]
    all_gather x3 -> x0, waiting for transfers between devices: 75.2 us -> none  [the longest x1 39.7 us: local(): query = lax.all_gather(query_part, 'grp', axis=1, tiled=True)]
    pallas_call x0 -> x1, Pallas kernels: none -> 43.4 us  [local(): pl.pallas_call(kernel, out_shape=(jax.ShapeDtypeStruct((1, ROWS, 2 * HD),...]
    all_gather x1 -> x0, blocking collectives: 27.8 us -> none  [local(): fresh = lax.all_gather(keyval_part, 'grp', axis=1, tiled=True)]
    dot_general x6 -> x0, matrix products: 24.8 us -> none  [the longest x1 7.3 us: token_parts(): jnp.einsum('rhgk,khd->rhgd', weights, val_heads, precision=lax.Precision....]
    mul x3 -> x0, other arithmetic: 12 us -> none  [the longest x1 12 us: local(): partial_value.reshape(row_count, HQ, HD) * factor[:, :, None]]
    reduce_sum x5 -> x0, other arithmetic: 6.52 us -> none  [the longest x1 3.71 us: token_parts(): total = jnp.sum(weights, axis=-1)]
  transfers between devices with their start and end apart: 5 -> 0, of which waited for: 3 -> 0; matrix products, arithmetic and copies ran while one was open for 5% -> 0% of each run, Pallas kernels for 0% -> 0%
where the time goes in v1:
time: 47.7 us; the launch traced here: 47.4 us
  Pallas kernels  43.4 us (91%)
  local copies, waits for them, and re-layouts  3.41 us (7%)
  between operations  0.64 us (1%)
    pallas_call x1, Pallas kernels, local(): pl.pallas_call(kernel, out_shape=(jax.ShapeDtypeStruct((1, ROWS, 2 * HD),...  43.4 us
    unnamed x2, local copies, waits for them, and re-layouts  3.41 us

profile of v1, /device:TPU:1, one launch (start us, length us, event | category | flops | bytes accessed | tf_op | source)
XLA Modules:
  0.0 47.4 jit_solution(390025028180266774)
XLA Ops:
  0.6 43.4 %joined_attention.1 = (bf16[1,160,256]{2,1,0:T(8,128)(2,1)}, bf16[8,16,2048]{2,1,0:T(8,128)(2,1)}) custom-call(bf16[1,160,8192]{2,1,0:T(8,128)(2,1)} %rows_hbm.1, f32[1,8192]{1,0:T(1,128)} %bitcast.3, bf16[8192,256]{1,0:T(8,128)(2,1)} %wq_hbm.1, bf16[64,8192]{1,0:T(8,128)(2,1)} %bitcast.2, bf16[8192,256]{1,0:T(8,128)(2,1)} %wo_hbm.1, ...), custom_call_target="tpu_custom_call" | custom-call | tf_op jit(solution)/shard_map/joined_attention/pallas_call | solution.py:486
  44.0 1.5 %copy.14 = bf16[1,160,256]{2,1,0:T(8,128)(2,1)} copy(bf16[1,160,256]{2,1,0:T(8,128)(2,1)} %get-tuple-element.4) | data formatting | bytes 163840
  45.6 1.9 %copy.15 = bf16[8,16,2048]{2,1,0:T(8,128)(2,1)} copy(bf16[8,16,2048]{2,1,0:T(8,128)(2,1)} %get-tuple-element.5) | data formatting | bytes 1048576

commit v2 on v1

--- a/solution.py
+++ b/solution.py
@@ -22,6 +22,10 @@
 NEG = -1e30
 FAR = 1e9
 LINE = (0, 1, 3, 2)
+HOPS = (0, 1, 2, 1)
+FARTHEST_FIRST = sorted(
+    [(n // 16, n // 4 % 4, n % 4) for n in range(1, 64)], key=lambda steps: -sum(HOPS[d] for d in steps)
+)
 
 
 def nt_dot(a, b):
@@ -55,7 +59,7 @@
     picked,
     qlen,
     out_ref,
-    joined_hbm,
+    joined_v,
     rows_v,
     gain_v,
     nrm,
@@ -63,9 +67,7 @@
     wk_v,
     wo_v,
     pool_v,
-    joined_v,
     sx,
-    rx,
     kv,
     kvp,
     fr,
@@ -81,8 +83,6 @@
     rj1,
     rj,
     ld,
-    xs_s,
-    xs_r,
     zs_s,
     zs_r,
     cs_s,
@@ -97,7 +97,6 @@
     g_r,
     gc_s,
     gc_r,
-    out_sem,
 ):
     r = lax.axis_index("req")
     m = lax.axis_index("grp")
@@ -121,26 +120,24 @@
     def wait_all(ref, sem):
         pltpu.make_async_copy(ref, ref, sem).wait()
 
+    barrier = pltpu.get_barrier_semaphore()
+
+    def others(act, first=0, last=63):
+        for dx, dy, dz in FARTHEST_FIRST[first:last]:
+            act(lax.rem(r + dx, 4), 4 * lax.rem(z + dz, 4) + lax.rem(y + dy, 4))
+
+    def greet(q, t):
+        pl.semaphore_signal(barrier, inc=1, device_id=(q, 2 * t + c), device_id_type=MESH)
+
+    others(greet)
+    pl.semaphore_signal(barrier, inc=1, device_id=sib, device_id_type=MESH)
+
     ld_pool = load(pool_hbm, pool_v, 0)
     ld_rows = [
         load(rows_hbm.at[0, pl.ds(32 * i, 32)], rows_v.at[pl.ds(32 * i, 32)], 1 + i) for i in range(5)
     ]
     ld_gain = load(gain_hbm, gain_v, 6)
     ld_wk = load(wk_hbm, wk_v.at[pl.ds(pl.multiple_of(64 * c, 64), 64)], 7)
-    ld_wq = [
-        load(wq_hbm.at[pl.ds(2048 * i, 2048)], wq_v.at[pl.ds(2048 * i, 2048)], 8 + i) for i in range(4)
-    ]
-    ld_wo = load(wo_hbm, wo_v, 12)
-
-    barrier = pltpu.get_barrier_semaphore()
-
-    def greet(d, carry):
-        pl.semaphore_signal(barrier, inc=1, device_id=(r, lax.rem(m + d, 32)), device_id_type=MESH)
-        return carry
-
-    lax.fori_loop(1, 32, greet, 0)
-    for d in range(1, 4):
-        pl.semaphore_signal(barrier, inc=1, device_id=(lax.rem(r + d, 4), m), device_id_type=MESH)
 
     wk_v[pl.ds(pl.multiple_of(64 - 64 * c, 64), 64), :] = jnp.zeros((64, D), BF16)
 
@@ -170,31 +167,13 @@
         piece = nn_dot(pick_page, pool_v[:, :, h * HD : (h + 1) * HD].reshape(128, HD)).astype(BF16)
         for q in range(4):
             sx[q, h % KVH, h // KVH] = piece[16 * q : 16 * (q + 1)]
-    pl.semaphore_wait(barrier, 34)
-    for d in (1, 3, 2):
-        q = lax.rem(r + d, 4)
-        push(sx.at[q], rx.at[r], xs_s.at[0], xs_r.at[d - 1], (q, m))
-
-    def spread(src, x):
-        def one(d, carry):
-            t = lax.rem(chip + d, 16)
-            push(
-                src.at[lax.div(t, 2)],
-                kv.at[c, chip, x],
-                zs_s.at[0],
-                zs_r.at[z],
-                (r, 2 * t + c),
-            )
-            return carry
-
-        pltpu.make_async_copy(src.at[k], kv.at[c, chip, x], zs_r.at[z]).start()
-        lax.fori_loop(1, 16, one, 0)
-
-    spread(sx.at[r], r)
-
     ld_gain.wait()
     for i in range(5):
         ld_rows[i].wait()
+
+    ld_wq = [
+        load(wq_hbm.at[pl.ds(2048 * i, 2048)], wq_v.at[pl.ds(2048 * i, 2048)], 8 + i) for i in range(4)
+    ]
 
     def norm(i, carry):
         at = pl.ds(pl.multiple_of(32 * i, 32), 32)
@@ -211,33 +190,34 @@
 
     lax.fori_loop(0, 5, norm, 0)
 
+    pl.semaphore_wait(barrier, 64)
+
+    def send_page(q, t):
+        push(sx.at[q, lax.div(t, 2)], kv.at[c, 16 * r + chip], zs_s.at[0], zs_r.at[r], (q, 2 * t + c))
+
+    pltpu.make_async_copy(sx.at[r, k], kv.at[c, 16 * r + chip], zs_r.at[r]).start()
+
     ld_wk.wait()
     part[0:ROWS, :] = jnp.zeros((ROWS, HD), F32)
 
-    def kv_step(i, carry):
-        cols = pl.ds(pl.multiple_of(1024 * i, 1024), 1024)
+    for i in range(8):
+        cols = slice(1024 * i, 1024 * (i + 1))
+        others(send_page, 8 * i, 8 * i + 8)
         part[0:ROWS, :] += nt_dot(nrm[:, cols], wk_v[:, cols])
-        return carry
-
-    lax.fori_loop(0, 8, kv_step, 0)
     kvp[...] = part[0:ROWS, :].astype(BF16)
+    ld_wo = load(wo_hbm, wo_v, 12)
     head_to = lax.div(lax.rem(m, 16), 2)
-    fr_slot = lax.div(m, 16) * 2 + c
-    for i in range(4):
-        t = 4 * head_to + i
-
-        @pl.when(t == m)
+    fr_slot = 2 * c + lax.div(m, 16)
+    for i in range(2):
+        t = 2 * head_to + i
+
+        @pl.when(t == chip)
         def _():
             pltpu.make_async_copy(kvp, fr.at[fr_slot], fr_r.at[0]).start()
 
-        @pl.when(t != m)
+        @pl.when(t != chip)
         def _():
-            push(kvp, fr.at[fr_slot], fr_s.at[0], fr_r.at[0], (r, t))
-
-    for d in (1, 3, 2):
-        x = lax.rem(r + 4 - d, 4)
-        wait_all(rx.at[x], xs_r.at[d - 1])
-        spread(rx.at[x], x)
+            push(kvp, fr.at[fr_slot], fr_s.at[0], fr_r.at[0], (r, 2 * t + c))
 
     acc[...] = jnp.zeros((ROWS, 2 * HD), F32)
     for i in range(4):
@@ -264,21 +244,29 @@
     row_pos_b = jnp.broadcast_to(row_pos, (ROWS, 256))
     picked_b = row_pos_b[0 : SPANS * RCH]
 
-    wait_all(fr, fr_r.at[0])
+    own_half = fr.at[pl.ds(2 * c, 2)]
+    wait_all(own_half, fr_r.at[0])
+    push(own_half, own_half, fr_s.at[1], fr_r.at[1], sib)
+    wait_all(fr.at[pl.ds(2 - 2 * c, 2)], fr_r.at[1])
     row = lax.broadcasted_iota(jnp.int32, (SPANS * RCH, 256), 0)
     wanted = by_index(lax.div(row, RCH), span_of) * RCH + lax.rem(row, RCH)
     pick_rows = jnp.where(lax.broadcasted_iota(jnp.int32, (SPANS * RCH, 256), 1) == wanted, 1.0, 0.0).astype(BF16)
     by_holder = []
     for s in range(2):
-        fk[s, 0:ROWS, :] = (fr[2 * s].astype(F32) + fr[2 * s + 1].astype(F32)).astype(BF16)
+        fk[s, 0:ROWS, :] = (fr[s].astype(F32) + fr[2 + s].astype(F32)).astype(BF16)
         fk[s, ROWS:256, :] = jnp.zeros((256 - ROWS, HD), BF16)
         by_holder.append(nn_dot(pick_rows, fk[s]))
     for x in range(4):
         sj[x] = jnp.concatenate([b[x * RCH : (x + 1) * RCH] for b in by_holder], axis=0).astype(BF16)
-    for d in (1, 3, 2):
-        x = lax.rem(r + d, 4)
-        push(sj.at[x], rj1.at[r], js_s.at[0], js_r.at[d - 1], (x, m))
-    rj1[r] = sj[r]
+    rj_half = lax.div(r, 2)
+    rj_slot = lax.rem(r, 2)
+
+    @pl.when(rj_half == c)
+    def _():
+        for d in (2, 1, 3):
+            x = lax.rem(r + d, 4)
+            push(sj.at[x], rj1.at[rj_slot], js_s.at[0], js_r.at[rj_slot], (x, m))
+        rj1[rj_slot] = sj[r]
 
     def score(at, keys, key_pos):
         s = nt_dot(q2[...], keys) * SCALE
@@ -293,48 +281,53 @@
     score(8, fk[0], fresh_pos)
 
     lane = lax.broadcasted_iota(jnp.int32, (1, 256), 1)
-    lane_x = (lane >> 4) & 3
-    span_lane = by_index(lane_x, span_of)
-    lane_pos = span_lane * 512 + (lane >> 6) * 32 + (lane & 15)
-
-    def page_keys(cc, zz):
-        pos = (lane_pos + (zz * 128 + cc * 16)).astype(F32)
+    lane_pos = (lane >> 4) * 32 + (lane & 15)
+
+    def page_keys(cc, x):
+        span = jnp.where(x == 0, span_of[0], jnp.where(x == 1, span_of[1], jnp.where(x == 2, span_of[2], span_of[3])))
+        pos = (lane_pos + (span * 512 + cc * 16)).astype(F32)
         same = picked_b == jnp.broadcast_to(pos, (SPANS * RCH, 256))
         gone = jnp.max(jnp.where(same, 1.0, 0.0), axis=0, keepdims=True)
         return jnp.where(gone > 0.5, FAR, pos)
 
-    for d in (0, 1, 3, 2):
-        zz = lax.rem(z + d, 4)
-        group = kv.at[c, pl.ds(4 * zz, 4)]
-        wait_all(group, zs_r.at[zz])
-        push(group, group, cs_s.at[0], cs_r.at[zz], sib)
-
-    def own_scores(zz, carry):
-        keys = kv[c, pl.ds(4 * zz, 4), :, 0].reshape(256, HD)
-        score(zz, keys, page_keys(c, zz))
+    def group(cc, x):
+        return kv.at[cc, pl.ds(16 * x, 16)]
+
+    for d in (2, 1, 3, 0):
+        x = lax.rem(r + d, 4)
+        wait_all(group(c, x), zs_r.at[x])
+        push(group(c, x), group(c, x), cs_s.at[0], cs_r.at[x], sib)
+
+    def page_part(cc, x, s):
+        return kv[cc, pl.ds(16 * x, 16), s].reshape(256, HD)
+
+    def own_scores(x, carry):
+        score(x, page_part(c, x, 0), page_keys(c, x))
         return carry
 
     lax.fori_loop(0, 4, own_scores, 0)
 
-    for d in (1, 3, 2):
-        x = lax.rem(r + 4 - d, 4)
-        wait_all(rj1.at[x], js_r.at[d - 1])
-    rj[k] = rj1[...]
+    def sib_scores(x, carry):
+        wait_all(group(1 - c, x), cs_r.at[x])
+        score(4 + x, page_part(1 - c, x, 0), page_keys(1 - c, x))
+        return carry
+
+    lax.fori_loop(0, 4, sib_scores, 0)
+
+    for q in range(2):
+
+        @pl.when(r != 2 * c + q)
+        def _():
+            wait_all(rj1.at[q], js_r.at[q])
+
+    rj[c, k] = rj1[...]
 
     def spread_fresh(d, carry):
         t = lax.rem(k + d, 8)
-        push(rj1, rj.at[k], jz_s.at[0], jz_r.at[0], (r, (2 * t + lax.rem(y, 2)) * 2 + c))
+        push(rj1, rj.at[c, k], jz_s.at[0], jz_r.at[0], (r, (2 * t + lax.rem(y, 2)) * 2 + c))
         return carry
 
     lax.fori_loop(1, 8, spread_fresh, 0)
-
-    def sib_scores(zz, carry):
-        wait_all(kv.at[1 - c, pl.ds(4 * zz, 4)], cs_r.at[zz])
-        keys = kv[1 - c, pl.ds(4 * zz, 4), :, 0].reshape(256, HD)
-        score(4 + zz, keys, page_keys(1 - c, zz))
-        return carry
-
-    lax.fori_loop(0, 4, sib_scores, 0)
 
     peak[...] = jnp.broadcast_to(jnp.max(peak[...], axis=1, keepdims=True), (2 * ROWS, 128))
     total[...] = jnp.zeros((2 * ROWS, 128), F32)
@@ -349,9 +342,7 @@
 
     def page_values(i, carry):
         far = lax.div(i, 4)
-        cc = c + far * (1 - 2 * c)
-        zz = lax.rem(i, 4)
-        weigh(i, kv[cc, pl.ds(4 * zz, 4), :, 1].reshape(256, HD))
+        weigh(i, page_part(c + far * (1 - 2 * c), lax.rem(i, 4), 1))
         return carry
 
     lax.fori_loop(0, 8, page_values, 0)
@@ -376,41 +367,48 @@
     def arrived(block):
         wait_all(gath.at[c, block], g_r.at[block])
 
-    def project(cc, ds, wait):
-        def one(df, carry):
+    def project(cc, ds):
+        more = jnp.zeros((ROWS, 2 * HD), F32)
+        for df in LINE:
             block = chip_at(cc, df, ds)
-            if wait:
-                wait_all(gath.at[cc, block], gc_r.at[block])
             at = pl.multiple_of((2 * block + cc) * 256, 256)
-            acc[...] += nn_dot(gath[cc, block], wo_v[pl.ds(at, 256), :])
-            return carry
-
-        lax.fori_loop(0, 4, one, 0)
-
-    for df, ds in ((1, 0), (3, 0), (2, 0), (0, 1), (0, 3)):
-        forward(chip, df, ds)
+            more = more + nn_dot(gath[cc, block], wo_v[pl.ds(at, 256), :])
+        acc[...] += more
+
+    def crossed(ds):
+        for df in LINE:
+            block = chip_at(1 - c, df, ds)
+            wait_all(gath.at[1 - c, block], gc_r.at[block])
+
+    for df in (2, 1, 3):
+        forward(chip, df, 0)
+    for ds in (2, 1, 3):
+        forward(chip, 0, ds)
     across(chip)
     acc[...] = jnp.zeros((ROWS, 2 * HD), F32)
+
     for df in (1, 3, 2):
         block = chip_at(c, df, 0)
         arrived(block)
-        forward(block, 0, 1)
-        forward(block, 0, 3)
+        for ds in (2, 1, 3) if df == 2 else (1, 3):
+            forward(block, 0, ds)
         across(block)
     ld_wo.wait()
-    project(c, 0, False)
-    for df in LINE:
-        for ds in (1, 3):
-            block = chip_at(c, df, ds)
-            arrived(block)
-            if (ds == 3) == (df in (0, 2)):
-                forward(block, 0, 4 - ds)
-            across(block)
-    project(1 - c, 0, True)
-    project(c, 1, False)
-    project(c, 3, False)
-
-    wait_all(rj.at[pl.ds(0, 7)], jz_r.at[0])
+    project(c, 0)
+    wait_all(rj.at[c, pl.ds(0, 7)], jz_r.at[0])
+    push(rj.at[c], rj.at[c], jz_s.at[1], jz_r.at[1], sib)
+    for df, ds in ((0, 1), (0, 3), (1, 3), (3, 1), (1, 1), (3, 3), (2, 1), (2, 3), (0, 2)):
+        block = chip_at(c, df, ds)
+        arrived(block)
+        if (df, ds) in ((1, 3), (3, 1)):
+            forward(block, 0, 4 - ds)
+        across(block)
+    crossed(0)
+    project(1 - c, 0)
+    project(c, 1)
+    project(c, 3)
+
+    wait_all(rj.at[1 - c], jz_r.at[1])
     col = lax.broadcasted_iota(jnp.int32, (RCH, 192), 1)
     col_req = lax.div(col, 48)
     col_in = lax.rem(col, 48)
@@ -436,44 +434,61 @@
     hit = jnp.broadcast_to(jnp.max(pick_key, axis=1, keepdims=True), (128, HD)) > 0.5
     pick = jnp.concatenate([pick_key, pick_val], axis=0).astype(BF16)
     for h in range(KVH):
-        new = nn_dot(pick, rj[h].reshape(192, HD))
+        new = nn_dot(pick[:, 0:96], rj[0, h].reshape(96, HD)) + nn_dot(pick[:, 96:192], rj[1, h].reshape(96, HD))
         for s in range(2):
             at = slice(1024 * s + h * HD, 1024 * s + (h + 1) * HD)
             old = pool_v[:, :, at].astype(F32).reshape(128, HD)
             joined_v[:, :, at] = (
                 jnp.where(hit, new[128 * s : 128 * (s + 1)], old).astype(BF16).reshape(8, 16, HD)
             )
-    joined_out = pltpu.make_async_copy(joined_v, joined_hbm, out_sem.at[0])
-    joined_out.start()
-
-    project(1 - c, 1, True)
-    project(1 - c, 3, True)
-    for df in LINE:
+
+    crossed(1)
+    project(1 - c, 1)
+    crossed(3)
+    project(1 - c, 3)
+    for df in (2, 1, 3):
         block = chip_at(c, df, 2)
         arrived(block)
         across(block)
-    project(c, 2, False)
-    project(1 - c, 2, True)
+    project(c, 2)
+    crossed(2)
+    project(1 - c, 2)
     live = lax.broadcasted_iota(jnp.int32, (ROWS, 2 * HD), 0) < SPANS * RCH + qlen[r]
     out_ref[0] = jnp.where(live, acc[...], 0.0).astype(BF16)
 
-    joined_out.wait()
-    wait_all(rx.at[pl.ds(0, 3)], xs_s.at[0])
-    wait_all(kv.at[0, pl.ds(0, 15)], zs_s.at[0])
+    wait_all(kv.at[0, pl.ds(0, 63)], zs_s.at[0])
     wait_all(kv.at[0], cs_s.at[0])
+
+    wait_all(own_half, fr_s.at[1])
 
     @pl.when(head_to == k)
     def _():
-        wait_all(fr.at[pl.ds(0, 3)], fr_s.at[0])
+        wait_all(fr.at[pl.ds(0, 1)], fr_s.at[0])
 
     @pl.when(head_to != k)
     def _():
-        wait_all(fr, fr_s.at[0])
-
-    wait_all(rj1.at[pl.ds(0, 3)], js_s.at[0])
-    wait_all(rj.at[pl.ds(0, 7)], jz_s.at[0])
+        wait_all(fr.at[pl.ds(0, 2)], fr_s.at[0])
+
+
+    @pl.when(rj_half == c)
+    def _():
+        wait_all(sj.at[pl.ds(0, 3)], js_s.at[0])
+
+    wait_all(rj.at[0, pl.ds(0, 7)], jz_s.at[0])
+    wait_all(rj.at[0], jz_s.at[1])
     wait_all(gath.at[0, pl.ds(0, 15)], g_s.at[0])
     wait_all(gath.at[0], gc_s.at[0])
+
+
+def finish(attn, joined, attn_out, joined_out, sems):
+    copies = [
+        pltpu.make_async_copy(joined, joined_out, sems.at[0]),
+        pltpu.make_async_copy(attn, attn_out, sems.at[1]),
+    ]
+    for cp in copies:
+        cp.start()
+    for cp in copies:
+        cp.wait()
 
 
 def local(
@@ -483,14 +498,11 @@
     smem = pl.BlockSpec(memory_space=pltpu.SMEM)
     vmem = pl.BlockSpec(memory_space=pltpu.VMEM)
     sem = pltpu.SemaphoreType.DMA
-    return pl.pallas_call(
+    attn, joined = pl.pallas_call(
         kernel,
-        out_shape=(
-            jax.ShapeDtypeStruct((1, ROWS, 2 * HD), BF16),
-            jax.ShapeDtypeStruct(page_pool.shape, BF16),
-        ),
+        out_shape=(pltpu.VMEM((1, ROWS, 2 * HD), BF16), pltpu.VMEM(page_pool.shape, BF16)),
         in_specs=[any_spec] * 6 + [smem, smem, vmem, smem],
-        out_specs=(vmem, any_spec),
+        out_specs=(vmem, vmem),
         scratch_shapes=[
             pltpu.VMEM((ROWS, D), BF16),
             pltpu.VMEM((1, D), F32),
@@ -499,10 +511,8 @@
             pltpu.VMEM((HD, D), BF16),
             pltpu.VMEM((D, 2 * HD), BF16),
             pltpu.VMEM((8, 16, 2048), BF16),
-            pltpu.VMEM((8, 16, 2048), BF16),
             pltpu.VMEM((4, KVH, 2, 16, HD), BF16),
-            pltpu.VMEM((4, KVH, 2, 16, HD), BF16),
-            pltpu.VMEM((2, 16, 4, 2, 16, HD), BF16),
+            pltpu.VMEM((2, 64, 2, 16, HD), BF16),
             pltpu.VMEM((ROWS, HD), BF16),
             pltpu.VMEM((4, ROWS, HD), BF16),
             pltpu.VMEM((2, 256, HD), BF16),
@@ -514,26 +524,23 @@
             pltpu.VMEM((2, 16, ROWS, 2 * HD), BF16),
             pltpu.VMEM((ROWS, 2 * HD), F32),
             pltpu.VMEM((4, 2 * RCH, HD), BF16),
-            pltpu.VMEM((4, 2 * RCH, HD), BF16),
-            pltpu.VMEM((KVH, 4, 2 * RCH, HD), BF16),
+            pltpu.VMEM((2, 2 * RCH, HD), BF16),
+            pltpu.VMEM((2, KVH, 2, 2 * RCH, HD), BF16),
             sem((13,)),
-            sem((1,)),
-            sem((3,)),
             sem((1,)),
             sem((4,)),
             sem((1,)),
             sem((4,)),
+            sem((2,)),
+            sem((2,)),
             sem((1,)),
-            sem((1,)),
-            sem((1,)),
-            sem((3,)),
-            sem((1,)),
-            sem((1,)),
+            sem((2,)),
+            sem((2,)),
+            sem((2,)),
             sem((1,)),
             sem((16,)),
             sem((1,)),
             sem((16,)),
-            sem((1,)),
         ],
         compiler_params=pltpu.CompilerParams(
             collective_id=0, has_side_effects=True, vmem_limit_bytes=56 * 1024 * 1024
@@ -551,6 +558,17 @@
         picked,
         question_len,
     )
+    return pl.pallas_call(
+        finish,
+        out_shape=(
+            jax.ShapeDtypeStruct(attn.shape, BF16),
+            jax.ShapeDtypeStruct(joined.shape, BF16),
+        ),
+        in_specs=[vmem, vmem],
+        out_specs=(any_spec, any_spec),
+        scratch_shapes=[sem((2,))],
+        name="write_out",
+    )(pltpu.with_memory_space_constraint(attn, pltpu.VMEM), pltpu.with_memory_space_constraint(joined, pltpu.VMEM))
 
 
 def solution(mesh):

time: 47.7 us -> 44.3 us (0.929)
  local copies, waits for them, and re-layouts: 3.41 us -> 0 us
    unnamed x2 -> x0, local copies, waits for them, and re-layouts: 3.41 us -> none
    pallas_call x1 -> x2, Pallas kernels: 43.4 us -> 43.5 us  [the longest x1 42.7 us: local(): pl.pallas_call(kernel, out_shape=(pltpu.VMEM((1, ROWS, 2 * HD), BF16), pl...]
where the time goes in v2:
time: 44.3 us; the launch traced here: 44.1 us
  Pallas kernels  43.5 us (98%)
  between operations  0.64 us (1%)
    pallas_call x1, Pallas kernels, local(): pl.pallas_call(kernel, out_shape=(pltpu.VMEM((1, ROWS, 2 * HD), BF16), pl...  42.7 us

profile of v2, /device:TPU:1, one launch (start us, length us, event | category | flops | bytes accessed | tf_op | source)
XLA Modules:
  0.0 44.1 jit_solution(14779964175362790035)
XLA Ops:
  0.6 42.7 %joined_attention.1 = (bf16[1,160,256]{2,1,0:T(8,128)(2,1)S(1)}, bf16[8,16,2048]{2,1,0:T(8,128)(2,1)S(1)}) custom-call(bf16[1,160,8192]{2,1,0:T(8,128)(2,1)} %rows_hbm.1, f32[1,8192]{1,0:T(1,128)} %bitcast.3, bf16[8192,256]{1,0:T(8,128)(2,1)} %wq_hbm.1, bf16[64,8192]{1,0:T(8,128)(2,1)} %bitcast.2, bf16[8192,256]{1,0:T(8,128)(2,1)} %wo_hbm.1, ...), custom_call_target="tpu_custom_call" | custom-call | tf_op jit(solution)/shard_map/joined_attention/pallas_call | solution.py:501
  43.3 0.8 %write_out.1 = (bf16[1,160,256]{2,1,0:T(8,128)(2,1)}, bf16[8,16,2048]{2,1,0:T(8,128)(2,1)}) custom-call(bf16[1,160,256]{2,1,0:T(8,128)(2,1)S(1)} %get-tuple-element.4.attn, bf16[8,16,2048]{2,1,0:T(8,128)(2,1)S(1)} %get-tuple-element.5.joined), custom_call_target="tpu_custom_call" | custom-call | tf_op jit(solution)/shard_map/write_out/pallas_call | solution.py:561

commit v3 on v2

--- a/solution.py
+++ b/solution.py
@@ -1,4 +1,5 @@
 import functools
+import math
 
 import jax
 import jax.numpy as jnp
@@ -18,7 +19,7 @@
 D = 8192
 KEYS = 2048
 EPS = 1e-05
-SCALE = 1.0 / float(HD) ** 0.5
+EXP2_SCALE = math.log2(math.e) / math.sqrt(HD)
 NEG = -1e30
 FAR = 1e9
 LINE = (0, 1, 3, 2)
@@ -75,8 +76,6 @@
     q2,
     scores,
     peak,
-    total,
-    part,
     gath,
     acc,
     sj,
@@ -132,11 +131,10 @@
     others(greet)
     pl.semaphore_signal(barrier, inc=1, device_id=sib, device_id_type=MESH)
 
+    for i in range(5):
+        load(rows_hbm.at[0, pl.ds(32 * i, 32)], rows_v.at[pl.ds(32 * i, 32)], 1 + i)
+    ld_gain = load(gain_hbm, gain_v, 6)
     ld_pool = load(pool_hbm, pool_v, 0)
-    ld_rows = [
-        load(rows_hbm.at[0, pl.ds(32 * i, 32)], rows_v.at[pl.ds(32 * i, 32)], 1 + i) for i in range(5)
-    ]
-    ld_gain = load(gain_hbm, gain_v, 6)
     ld_wk = load(wk_hbm, wk_v.at[pl.ds(pl.multiple_of(64 * c, 64), 64)], 7)
 
     wk_v[pl.ds(pl.multiple_of(64 - 64 * c, 64), 64), :] = jnp.zeros((64, D), BF16)
@@ -168,15 +166,10 @@
         for q in range(4):
             sx[q, h % KVH, h // KVH] = piece[16 * q : 16 * (q + 1)]
     ld_gain.wait()
-    for i in range(5):
-        ld_rows[i].wait()
-
-    ld_wq = [
-        load(wq_hbm.at[pl.ds(2048 * i, 2048)], wq_v.at[pl.ds(2048 * i, 2048)], 8 + i) for i in range(4)
-    ]
 
     def norm(i, carry):
         at = pl.ds(pl.multiple_of(32 * i, 32), 32)
+        wait_all(rows_v.at[at], ld.at[1 + i])
         squares = jnp.zeros((32, 128), F32)
         for j in range(D // 128):
             v = rows_v[at, j * 128 : (j + 1) * 128].astype(F32)
@@ -190,22 +183,17 @@
 
     lax.fori_loop(0, 5, norm, 0)
 
-    pl.semaphore_wait(barrier, 64)
-
-    def send_page(q, t):
-        push(sx.at[q, lax.div(t, 2)], kv.at[c, 16 * r + chip], zs_s.at[0], zs_r.at[r], (q, 2 * t + c))
-
-    pltpu.make_async_copy(sx.at[r, k], kv.at[c, 16 * r + chip], zs_r.at[r]).start()
+    ld_wq = [
+        load(wq_hbm.at[pl.ds(1024 * i, 1024)], wq_v.at[pl.ds(1024 * i, 1024)], 8 + i) for i in range(8)
+    ]
 
     ld_wk.wait()
-    part[0:ROWS, :] = jnp.zeros((ROWS, HD), F32)
-
+    new_kv = jnp.zeros((ROWS, HD), F32)
     for i in range(8):
         cols = slice(1024 * i, 1024 * (i + 1))
-        others(send_page, 8 * i, 8 * i + 8)
-        part[0:ROWS, :] += nt_dot(nrm[:, cols], wk_v[:, cols])
-    kvp[...] = part[0:ROWS, :].astype(BF16)
-    ld_wo = load(wo_hbm, wo_v, 12)
+        new_kv = new_kv + nt_dot(nrm[:, cols], wk_v[:, cols])
+    kvp[...] = new_kv.astype(BF16)
+    pl.semaphore_wait(barrier, 64)
     head_to = lax.div(lax.rem(m, 16), 2)
     fr_slot = 2 * c + lax.div(m, 16)
     for i in range(2):
@@ -219,18 +207,24 @@
         def _():
             push(kvp, fr.at[fr_slot], fr_s.at[0], fr_r.at[0], (r, 2 * t + c))
 
-    acc[...] = jnp.zeros((ROWS, 2 * HD), F32)
-    for i in range(4):
+    def send_page(q, t):
+        push(sx.at[q, lax.div(t, 2)], kv.at[c, 16 * r + chip], zs_s.at[0], zs_r.at[r], (q, 2 * t + c))
+
+    pltpu.make_async_copy(sx.at[r, k], kv.at[c, 16 * r + chip], zs_r.at[r]).start()
+
+    pl.when(m >= 0)(functools.partial(others, send_page))
+    query = jnp.zeros((ROWS, 2 * HD), F32)
+    for i in range(8):
         ld_wq[i].wait()
-
-        def q_step(j, carry):
-            at = pl.multiple_of(2048 * i + 1024 * j, 1024)
-            acc[...] += nn_dot(nrm[:, pl.ds(at, 1024)], wq_v[pl.ds(at, 1024), :])
-            return carry
-
-        lax.fori_loop(0, 2, q_step, 0)
-    q2[0:ROWS, :] = acc[:, 0:HD].astype(BF16)
-    q2[ROWS : 2 * ROWS, :] = acc[:, HD : 2 * HD].astype(BF16)
+        at = slice(1024 * i, 1024 * (i + 1))
+        query = query + nn_dot(nrm[:, at], wq_v[at, :])
+    q2[0:ROWS, :] = query[:, 0:HD].astype(BF16)
+    q2[ROWS : 2 * ROWS, :] = query[:, HD : 2 * HD].astype(BF16)
+
+    own_half = fr.at[pl.ds(2 * c, 2)]
+    wait_all(own_half, fr_r.at[0])
+    push(own_half, own_half, fr_s.at[1], fr_r.at[1], sib)
+    ld_wo = load(wo_hbm, wo_v, 16)
 
     own_picked = picked[r].astype(F32)
     cols = [to_column(own_picked[s : s + 1, :]) + 512.0 * s for s in range(SPANS)]
@@ -244,9 +238,6 @@
     row_pos_b = jnp.broadcast_to(row_pos, (ROWS, 256))
     picked_b = row_pos_b[0 : SPANS * RCH]
 
-    own_half = fr.at[pl.ds(2 * c, 2)]
-    wait_all(own_half, fr_r.at[0])
-    push(own_half, own_half, fr_s.at[1], fr_r.at[1], sib)
     wait_all(fr.at[pl.ds(2 - 2 * c, 2)], fr_r.at[1])
     row = lax.broadcasted_iota(jnp.int32, (SPANS * RCH, 256), 0)
     wanted = by_index(lax.div(row, RCH), span_of) * RCH + lax.rem(row, RCH)
@@ -269,7 +260,7 @@
         rj1[rj_slot] = sj[r]
 
     def score(at, keys, key_pos):
-        s = nt_dot(q2[...], keys) * SCALE
+        s = nt_dot(q2[...], keys)
         seen = row_pos_b >= jnp.broadcast_to(key_pos, (ROWS, 256))
         for half in range(2):
             rows = slice(half * ROWS, (half + 1) * ROWS)
@@ -280,6 +271,29 @@
     peak[...] = jnp.full((2 * ROWS, 128), NEG, F32)
     score(8, fk[0], fresh_pos)
 
+    def group(cc, x):
+        return kv.at[cc, pl.ds(16 * x, 16)]
+
+    for d in (2, 1, 3, 0):
+        x = lax.rem(r + d, 4)
+        wait_all(group(c, x), zs_r.at[x])
+        push(group(c, x), group(c, x), cs_s.at[0], cs_r.at[x], sib)
+
+    for q in range(2):
+
+        @pl.when(r != 2 * c + q)
+        def _():
+            wait_all(rj1.at[q], js_r.at[q])
+
+    rj[c, k] = rj1[...]
+
+    def spread_fresh(d, carry):
+        t = lax.rem(k + d, 8)
+        push(rj1, rj.at[c, k], jz_s.at[0], jz_r.at[0], (r, (2 * t + lax.rem(y, 2)) * 2 + c))
+        return carry
+
+    lax.fori_loop(1, 8, spread_fresh, 0)
+
     lane = lax.broadcasted_iota(jnp.int32, (1, 256), 1)
     lane_pos = (lane >> 4) * 32 + (lane & 15)
 
@@ -290,66 +304,29 @@
         gone = jnp.max(jnp.where(same, 1.0, 0.0), axis=0, keepdims=True)
         return jnp.where(gone > 0.5, FAR, pos)
 
-    def group(cc, x):
-        return kv.at[cc, pl.ds(16 * x, 16)]
-
-    for d in (2, 1, 3, 0):
-        x = lax.rem(r + d, 4)
-        wait_all(group(c, x), zs_r.at[x])
-        push(group(c, x), group(c, x), cs_s.at[0], cs_r.at[x], sib)
-
     def page_part(cc, x, s):
         return kv[cc, pl.ds(16 * x, 16), s].reshape(256, HD)
 
-    def own_scores(x, carry):
-        score(x, page_part(c, x, 0), page_keys(c, x))
-        return carry
-
-    lax.fori_loop(0, 4, own_scores, 0)
-
-    def sib_scores(x, carry):
+    for x in range(4):
+        score(4 * c + x, page_part(c, x, 0), page_keys(c, x))
+
+    for x in range(4):
         wait_all(group(1 - c, x), cs_r.at[x])
-        score(4 + x, page_part(1 - c, x, 0), page_keys(1 - c, x))
-        return carry
-
-    lax.fori_loop(0, 4, sib_scores, 0)
-
-    for q in range(2):
-
-        @pl.when(r != 2 * c + q)
-        def _():
-            wait_all(rj1.at[q], js_r.at[q])
-
-    rj[c, k] = rj1[...]
-
-    def spread_fresh(d, carry):
-        t = lax.rem(k + d, 8)
-        push(rj1, rj.at[c, k], jz_s.at[0], jz_r.at[0], (r, (2 * t + lax.rem(y, 2)) * 2 + c))
-        return carry
-
-    lax.fori_loop(1, 8, spread_fresh, 0)
-
-    peak[...] = jnp.broadcast_to(jnp.max(peak[...], axis=1, keepdims=True), (2 * ROWS, 128))
-    total[...] = jnp.zeros((2 * ROWS, 128), F32)
-    part[...] = jnp.zeros((2 * ROWS, HD), F32)
-
-    def weigh(at, vals):
-        top = peak[...]
-        w0 = jnp.exp(scores[at, :, 0:128] - top)
-        w1 = jnp.exp(scores[at, :, 128:256] - top)
-        total[...] += w0 + w1
-        part[...] += nn_dot(jnp.concatenate([w0, w1], axis=1).astype(BF16), vals)
-
-    def page_values(i, carry):
-        far = lax.div(i, 4)
-        weigh(i, page_part(c + far * (1 - 2 * c), lax.rem(i, 4), 1))
-        return carry
-
-    lax.fori_loop(0, 8, page_values, 0)
-    weigh(8, fk[1])
-    att = part[...] / jnp.sum(total[...], axis=1, keepdims=True)
-    gath[c, chip, :, 0:HD] = att[0:ROWS].astype(BF16)
-    gath[c, chip, :, HD : 2 * HD] = att[ROWS : 2 * ROWS].astype(BF16)
+        score(4 * (1 - c) + x, page_part(1 - c, x, 0), page_keys(1 - c, x))
+
+    for h in range(2):
+        rows = slice(h * ROWS, (h + 1) * ROWS)
+        top = jnp.broadcast_to(jnp.max(peak[rows, :], axis=1, keepdims=True), (ROWS, 128))
+        total = jnp.zeros((ROWS, 128), F32)
+        mixed = jnp.zeros((ROWS, HD), F32)
+        for i in range(9):
+            w0 = jnp.exp2((scores[i, rows, 0:128] - top) * EXP2_SCALE)
+            w1 = jnp.exp2((scores[i, rows, 128:256] - top) * EXP2_SCALE)
+            total = total + (w0 + w1)
+            vals = fk[1] if i == 8 else page_part(i // 4, i % 4, 1)
+            mixed = mixed + nn_dot(jnp.concatenate([w0, w1], axis=1).astype(BF16), vals)
+        att = mixed / jnp.sum(total, axis=1, keepdims=True)
+        gath[c, chip, :, h * HD : (h + 1) * HD] = att.astype(BF16)
 
     def chip_at(cc, df, ds):
         f = lax.rem(y * (1 - cc) + z * cc + df, 4)
@@ -380,23 +357,22 @@
             block = chip_at(1 - c, df, ds)
             wait_all(gath.at[1 - c, block], gc_r.at[block])
 
-    for df in (2, 1, 3):
+    for df in (1, 3, 2):
         forward(chip, df, 0)
-    for ds in (2, 1, 3):
+    across(chip)
+    for ds in (1, 3):
         forward(chip, 0, ds)
-    across(chip)
     acc[...] = jnp.zeros((ROWS, 2 * HD), F32)
-
     for df in (1, 3, 2):
         block = chip_at(c, df, 0)
         arrived(block)
         for ds in (2, 1, 3) if df == 2 else (1, 3):
             forward(block, 0, ds)
         across(block)
+        if df == 3:
+            forward(chip, 0, 2)
     ld_wo.wait()
     project(c, 0)
-    wait_all(rj.at[c, pl.ds(0, 7)], jz_r.at[0])
-    push(rj.at[c], rj.at[c], jz_s.at[1], jz_r.at[1], sib)
     for df, ds in ((0, 1), (0, 3), (1, 3), (3, 1), (1, 1), (3, 3), (2, 1), (2, 3), (0, 2)):
         block = chip_at(c, df, ds)
         arrived(block)
@@ -404,10 +380,21 @@
             forward(block, 0, 4 - ds)
         across(block)
     crossed(0)
+    wait_all(rj.at[c, pl.ds(0, 7)], jz_r.at[0])
+    push(rj.at[c], rj.at[c], jz_s.at[1], jz_r.at[1], sib)
     project(1 - c, 0)
     project(c, 1)
     project(c, 3)
 
+    crossed(1)
+    project(1 - c, 1)
+    crossed(3)
+    project(1 - c, 3)
+    for df in (2, 1, 3):
+        block = chip_at(c, df, 2)
+        arrived(block)
+        across(block)
+    project(c, 2)
     wait_all(rj.at[1 - c], jz_r.at[1])
     col = lax.broadcasted_iota(jnp.int32, (RCH, 192), 1)
     col_req = lax.div(col, 48)
@@ -442,15 +429,6 @@
                 jnp.where(hit, new[128 * s : 128 * (s + 1)], old).astype(BF16).reshape(8, 16, HD)
             )
 
-    crossed(1)
-    project(1 - c, 1)
-    crossed(3)
-    project(1 - c, 3)
-    for df in (2, 1, 3):
-        block = chip_at(c, df, 2)
-        arrived(block)
-        across(block)
-    project(c, 2)
     crossed(2)
     project(1 - c, 2)
     live = lax.broadcasted_iota(jnp.int32, (ROWS, 2 * HD), 0) < SPANS * RCH + qlen[r]
@@ -519,14 +497,12 @@
             pltpu.VMEM((2 * ROWS, HD), BF16),
             pltpu.VMEM((9, 2 * ROWS, 256), F32),
             pltpu.VMEM((2 * ROWS, 128), F32),
-            pltpu.VMEM((2 * ROWS, 128), F32),
-            pltpu.VMEM((2 * ROWS, HD), F32),
             pltpu.VMEM((2, 16, ROWS, 2 * HD), BF16),
             pltpu.VMEM((ROWS, 2 * HD), F32),
             pltpu.VMEM((4, 2 * RCH, HD), BF16),
             pltpu.VMEM((2, 2 * RCH, HD), BF16),
             pltpu.VMEM((2, KVH, 2, 2 * RCH, HD), BF16),
-            sem((13,)),
+            sem((17,)),
             sem((1,)),
             sem((4,)),
             sem((1,)),

time: 44.3 us -> 41.8 us (0.944)
  Pallas kernels: 43.5 us -> 41 us
    pallas_call x1, Pallas kernels: 42.7 us -> 40.2 us  [local(): pl.pallas_call(kernel, out_shape=(pltpu.VMEM((1, ROWS, 2 * HD), BF16), pl...]
where the time goes in v3:
time: 41.8 us; the launch traced here: 41.7 us
  Pallas kernels  41 us (98%)
  between operations  0.64 us (2%)
    pallas_call x1, Pallas kernels, local(): pl.pallas_call(kernel, out_shape=(pltpu.VMEM((1, ROWS, 2 * HD), BF16), pl...  40.2 us

profile of v3, /device:TPU:1, one launch (start us, length us, event | category | flops | bytes accessed | tf_op | source)
XLA Modules:
  0.0 41.7 jit_solution(16278180129190662736)
XLA Ops:
  0.6 40.2 %joined_attention.1 = (bf16[1,160,256]{2,1,0:T(8,128)(2,1)S(1)}, bf16[8,16,2048]{2,1,0:T(8,128)(2,1)S(1)}) custom-call(bf16[1,160,8192]{2,1,0:T(8,128)(2,1)} %rows_hbm.1, f32[1,8192]{1,0:T(1,128)} %bitcast.3, bf16[8192,256]{1,0:T(8,128)(2,1)} %wq_hbm.1, bf16[64,8192]{1,0:T(8,128)(2,1)} %bitcast.2, bf16[8192,256]{1,0:T(8,128)(2,1)} %wo_hbm.1, ...), custom_call_target="tpu_custom_call" | custom-call | tf_op jit(solution)/shard_map/joined_attention/pallas_call | solution.py:479
  40.8 0.8 %write_out.1 = (bf16[1,160,256]{2,1,0:T(8,128)(2,1)}, bf16[8,16,2048]{2,1,0:T(8,128)(2,1)}) custom-call(bf16[1,160,256]{2,1,0:T(8,128)(2,1)S(1)} %get-tuple-element.4.attn, bf16[8,16,2048]{2,1,0:T(8,128)(2,1)S(1)} %get-tuple-element.5.joined), custom_call_target="tpu_custom_call" | custom-call | tf_op jit(solution)/shard_map/write_out/pallas_call | solution.py:537

commit v4 on v3

--- a/solution.py
+++ b/solution.py
@@ -55,12 +55,16 @@
     wk_hbm,
     wo_hbm,
     pool_hbm,
+    ids_hbm,
+    slots_hbm,
+    picked_hbm,
+    qlen_hbm,
+    out_ref,
+    joined_v,
     ids,
     slots,
     picked,
     qlen,
-    out_ref,
-    joined_v,
     rows_v,
     gain_v,
     nrm,
@@ -131,6 +135,12 @@
     others(greet)
     pl.semaphore_signal(barrier, inc=1, device_id=sib, device_id_type=MESH)
 
+    ld_small = [
+        load(ids_hbm, ids, 17),
+        load(slots_hbm, slots, 18),
+        load(qlen_hbm, qlen, 19),
+        load(picked_hbm, picked, 20),
+    ]
     for i in range(5):
         load(rows_hbm.at[0, pl.ds(32 * i, 32)], rows_v.at[pl.ds(32 * i, 32)], 1 + i)
     ld_gain = load(gain_hbm, gain_v, 6)
@@ -139,6 +149,8 @@
 
     wk_v[pl.ds(pl.multiple_of(64 - 64 * c, 64), 64), :] = jnp.zeros((64, D), BF16)
 
+    for cp in ld_small:
+        cp.wait()
     place = [[slots[ids[q, s]] for s in range(SPANS)] for q in range(4)]
     send_slot, send_span = [], []
     for q in range(4):
@@ -473,15 +485,18 @@
     rows_in, norm_gain, w_query, w_keyval, w_out, page_pool, stretch_ids, page_slot, picked, question_len
 ):
     any_spec = pl.BlockSpec(memory_space=pl.ANY)
-    smem = pl.BlockSpec(memory_space=pltpu.SMEM)
     vmem = pl.BlockSpec(memory_space=pltpu.VMEM)
     sem = pltpu.SemaphoreType.DMA
     attn, joined = pl.pallas_call(
         kernel,
         out_shape=(pltpu.VMEM((1, ROWS, 2 * HD), BF16), pltpu.VMEM(page_pool.shape, BF16)),
-        in_specs=[any_spec] * 6 + [smem, smem, vmem, smem],
+        in_specs=[any_spec] * 10,
         out_specs=(vmem, vmem),
         scratch_shapes=[
+            pltpu.SMEM((4, SPANS), jnp.int32),
+            pltpu.SMEM((32,), jnp.int32),
+            pltpu.VMEM((4, SPANS, RCH), jnp.int32),
+            pltpu.SMEM((4,), jnp.int32),
             pltpu.VMEM((ROWS, D), BF16),
             pltpu.VMEM((1, D), F32),
             pltpu.VMEM((ROWS, D), BF16),
@@ -502,7 +517,7 @@
             pltpu.VMEM((4, 2 * RCH, HD), BF16),
             pltpu.VMEM((2, 2 * RCH, HD), BF16),
             pltpu.VMEM((2, KVH, 2, 2 * RCH, HD), BF16),
-            sem((17,)),
+            sem((21,)),
             sem((1,)),
             sem((4,)),
             sem((1,)),

time: 41.8 us -> 41.1 us (0.983)
  Pallas kernels: 41 us -> 40.3 us
    pallas_call x1, Pallas kernels: 40.2 us -> 39.5 us  [local(): pl.pallas_call(kernel, out_shape=(pltpu.VMEM((1, ROWS, 2 * HD), BF16), pl...]
where the time goes in v4:
time: 41.1 us; the launch traced here: 41 us
  Pallas kernels  40.3 us (98%)
  between operations  0.64 us (2%)
    pallas_call x1, Pallas kernels, local(): pl.pallas_call(kernel, out_shape=(pltpu.VMEM((1, ROWS, 2 * HD), BF16), pl...  39.5 us
    pallas_call x1, Pallas kernels, local(): pl.pallas_call(finish, out_shape=(jax.ShapeDtypeStruct(attn.shape, BF16),...  0.83 us

profile of v4, /device:TPU:1, one launch (start us, length us, event | category | flops | bytes accessed | tf_op | source)
XLA Modules:
  0.0 41.0 jit_solution(674828514291698671)
XLA Ops:
  0.6 39.5 %joined_attention.1 = (bf16[1,160,256]{2,1,0:T(8,128)(2,1)S(1)}, bf16[8,16,2048]{2,1,0:T(8,128)(2,1)S(1)}) custom-call(bf16[1,160,8192]{2,1,0:T(8,128)(2,1)} %rows_hbm.1, f32[1,8192]{1,0:T(1,128)} %bitcast.3, bf16[8192,256]{1,0:T(8,128)(2,1)} %wq_hbm.1, bf16[64,8192]{1,0:T(8,128)(2,1)} %bitcast.2, bf16[8192,256]{1,0:T(8,128)(2,1)} %wo_hbm.1, ...), custom_call_target="tpu_custom_call" | custom-call | tf_op jit(solution)/shard_map/joined_attention/pallas_call | solution.py:490
  40.1 0.8 %write_out.1 = (bf16[1,160,256]{2,1,0:T(8,128)(2,1)}, bf16[8,16,2048]{2,1,0:T(8,128)(2,1)}) custom-call(bf16[1,160,256]{2,1,0:T(8,128)(2,1)S(1)} %get-tuple-element.4.attn, bf16[8,16,2048]{2,1,0:T(8,128)(2,1)S(1)} %get-tuple-element.5.joined), custom_call_target="tpu_custom_call" | custom-call | tf_op jit(solution)/shard_map/write_out/pallas_call | solution.py:552

commit v5 on v4

--- a/solution.py
+++ b/solution.py
@@ -146,6 +146,9 @@
     ld_gain = load(gain_hbm, gain_v, 6)
     ld_pool = load(pool_hbm, pool_v, 0)
     ld_wk = load(wk_hbm, wk_v.at[pl.ds(pl.multiple_of(64 * c, 64), 64)], 7)
+    ld_wq = [
+        load(wq_hbm.at[pl.ds(1024 * i, 1024)], wq_v.at[pl.ds(1024 * i, 1024)], 8 + i) for i in range(8)
+    ]
 
     wk_v[pl.ds(pl.multiple_of(64 - 64 * c, 64), 64), :] = jnp.zeros((64, D), BF16)
 
@@ -195,9 +198,6 @@
 
     lax.fori_loop(0, 5, norm, 0)
 
-    ld_wq = [
-        load(wq_hbm.at[pl.ds(1024 * i, 1024)], wq_v.at[pl.ds(1024 * i, 1024)], 8 + i) for i in range(8)
-    ]
 
     ld_wk.wait()
     new_kv = jnp.zeros((ROWS, HD), F32)
@@ -236,7 +236,6 @@
     own_half = fr.at[pl.ds(2 * c, 2)]
     wait_all(own_half, fr_r.at[0])
     push(own_half, own_half, fr_s.at[1], fr_r.at[1], sib)
-    ld_wo = load(wo_hbm, wo_v, 16)
 
     own_picked = picked[r].astype(F32)
     cols = [to_column(own_picked[s : s + 1, :]) + 512.0 * s for s in range(SPANS)]
@@ -306,6 +305,7 @@
 
     lax.fori_loop(1, 8, spread_fresh, 0)
 
+    ld_wo = load(wo_hbm, wo_v, 16)
     lane = lax.broadcasted_iota(jnp.int32, (1, 256), 1)
     lane_pos = (lane >> 4) * 32 + (lane & 15)
 
@@ -381,14 +381,12 @@
         for ds in (2, 1, 3) if df == 2 else (1, 3):
             forward(block, 0, ds)
         across(block)
-        if df == 3:
-            forward(chip, 0, 2)
     ld_wo.wait()
     project(c, 0)
     for df, ds in ((0, 1), (0, 3), (1, 3), (3, 1), (1, 1), (3, 3), (2, 1), (2, 3), (0, 2)):
         block = chip_at(c, df, ds)
         arrived(block)
-        if (df, ds) in ((1, 3), (3, 1)):
+        if (df, ds) in ((0, 1), (1, 3), (3, 1)):
             forward(block, 0, 4 - ds)
         across(block)
     crossed(0)

time: 41.1 us -> 40.5 us (0.985)
  Pallas kernels: 40.3 us -> 39.7 us
    pallas_call x1, Pallas kernels: 39.5 us -> 38.9 us  [local(): pl.pallas_call(kernel, out_shape=(pltpu.VMEM((1, ROWS, 2 * HD), BF16), pl...]
where the time goes in v5:
time: 40.5 us; the launch traced here: 40.4 us
  Pallas kernels  39.7 us (98%)
  between operations  0.64 us (2%)
    pallas_call x1, Pallas kernels, local(): pl.pallas_call(kernel, out_shape=(pltpu.VMEM((1, ROWS, 2 * HD), BF16), pl...  38.9 us
    pallas_call x1, Pallas kernels, local(): pl.pallas_call(finish, out_shape=(jax.ShapeDtypeStruct(attn.shape, BF16),...  0.83 us

profile of v5, /device:TPU:1, one launch (start us, length us, event | category | flops | bytes accessed | tf_op | source)
XLA Modules:
  0.0 40.4 jit_solution(5610743186434390958)
XLA Ops:
  0.6 38.9 %joined_attention.1 = (bf16[1,160,256]{2,1,0:T(8,128)(2,1)S(1)}, bf16[8,16,2048]{2,1,0:T(8,128)(2,1)S(1)}) custom-call(bf16[1,160,8192]{2,1,0:T(8,128)(2,1)} %rows_hbm.1, f32[1,8192]{1,0:T(1,128)} %bitcast.3, bf16[8192,256]{1,0:T(8,128)(2,1)} %wq_hbm.1, bf16[64,8192]{1,0:T(8,128)(2,1)} %bitcast.2, bf16[8192,256]{1,0:T(8,128)(2,1)} %wo_hbm.1, ...), custom_call_target="tpu_custom_call" | custom-call | tf_op jit(solution)/shard_map/joined_attention/pallas_call | solution.py:488
  39.5 0.8 %write_out.1 = (bf16[1,160,256]{2,1,0:T(8,128)(2,1)}, bf16[8,16,2048]{2,1,0:T(8,128)(2,1)}) custom-call(bf16[1,160,256]{2,1,0:T(8,128)(2,1)S(1)} %get-tuple-element.4.attn, bf16[8,16,2048]{2,1,0:T(8,128)(2,1)S(1)} %get-tuple-element.5.joined), custom_call_target="tpu_custom_call" | custom-call | tf_op jit(solution)/shard_map/write_out/pallas_call | solution.py:550

commit v6 on v5

--- a/solution.py
+++ b/solution.py
@@ -24,8 +24,8 @@
 FAR = 1e9
 LINE = (0, 1, 3, 2)
 HOPS = (0, 1, 2, 1)
-FARTHEST_FIRST = sorted(
-    [(n // 16, n // 4 % 4, n % 4) for n in range(1, 64)], key=lambda steps: -sum(HOPS[d] for d in steps)
+NEAREST_FIRST = sorted(
+    [(n // 16, n // 4 % 4, n % 4) for n in range(1, 64)], key=lambda steps: sum(HOPS[d] for d in steps)
 )
 
 
@@ -126,7 +126,7 @@
     barrier = pltpu.get_barrier_semaphore()
 
     def others(act, first=0, last=63):
-        for dx, dy, dz in FARTHEST_FIRST[first:last]:
+        for dx, dy, dz in NEAREST_FIRST[first:last]:
             act(lax.rem(r + dx, 4), 4 * lax.rem(z + dz, 4) + lax.rem(y + dy, 4))
 
     def greet(q, t):

time: 40.5 us -> 40.3 us (level)
  no operation moved by 1% of the time
where the time goes in v6:
time: 40.3 us; the launch traced here: 40.2 us
  Pallas kernels  39.6 us (98%)
  between operations  0.64 us (2%)
    pallas_call x1, Pallas kernels, local(): pl.pallas_call(kernel, out_shape=(pltpu.VMEM((1, ROWS, 2 * HD), BF16), pl...  38.8 us
    pallas_call x1, Pallas kernels, local(): pl.pallas_call(finish, out_shape=(jax.ShapeDtypeStruct(attn.shape, BF16),...  0.83 us

profile of v6, /device:TPU:1, one launch (start us, length us, event | category | flops | bytes accessed | tf_op | source)
XLA Modules:
  0.0 40.2 jit_solution(8573621797208808641)
XLA Ops:
  0.6 38.8 %joined_attention.1 = (bf16[1,160,256]{2,1,0:T(8,128)(2,1)S(1)}, bf16[8,16,2048]{2,1,0:T(8,128)(2,1)S(1)}) custom-call(bf16[1,160,8192]{2,1,0:T(8,128)(2,1)} %rows_hbm.1, f32[1,8192]{1,0:T(1,128)} %bitcast.3, bf16[8192,256]{1,0:T(8,128)(2,1)} %wq_hbm.1, bf16[64,8192]{1,0:T(8,128)(2,1)} %bitcast.2, bf16[8192,256]{1,0:T(8,128)(2,1)} %wo_hbm.1, ...), custom_call_target="tpu_custom_call" | custom-call | tf_op jit(solution)/shard_map/joined_attention/pallas_call | solution.py:488
  39.4 0.8 %write_out.1 = (bf16[1,160,256]{2,1,0:T(8,128)(2,1)}, bf16[8,16,2048]{2,1,0:T(8,128)(2,1)}) custom-call(bf16[1,160,256]{2,1,0:T(8,128)(2,1)S(1)} %get-tuple-element.4.attn, bf16[8,16,2048]{2,1,0:T(8,128)(2,1)S(1)} %get-tuple-element.5.joined), custom_call_target="tpu_custom_call" | custom-call | tf_op jit(solution)/shard_map/write_out/pallas_call | solution.py:550
